TPU v7x, 128 devices: a whole 4x4x4 slice. The times are simulated.
128 devices in a mesh: lat: 4 (over y_hi, core), lon: 32 (over y_lo, x, z).
Axes of the slice: x: 4, y: 4 (y_hi: 2, y_lo: 2; y = y_hi * 2 + y_lo), z: 4, core: 2. Of those that a mesh axis runs over, the one named last changes fastest.
Arguments:
- tokens: bfloat16 [2, 24, 768, 512], P(None, 'lat', 'lon'), may hold values from -6 to 6
- cotangent: bfloat16 [2, 24, 768, 512], P(None, 'lat', 'lon'), may hold values from -6 to 6
- key_keep: int32 [2, 24, 768], P(None, 'lat', 'lon'), may hold values 0 or 1
- norm_gain: float32 [512], replicated, may hold values from 0.5 to 1.5
- w_qkv: bfloat16 [512, 1536], replicated, may hold values from -0.25 to 0.25
- w_proj: bfloat16 [512, 512], replicated, may hold values from -0.25 to 0.25
- attn_scale: float32 [8], replicated, may hold values from 1 to 10
Outputs:
- mixed: bfloat16 [2, 24, 768, 512], P(None, 'lat', 'lon')
- grad_tokens: bfloat16 [2, 24, 768, 512], P(None, 'lat', 'lon')
- grad_qkv: float32 [512, 1536], replicated
- grad_proj: float32 [512, 512], replicated
- grad_gain: float32 [512], replicated
- grad_scale: float32 [8], replicated
Inputs may be any that keep to these rules, and one draw needn't show every extreme that they name: `key_keep`: 1 marks a token that may serve as a key, 0 a padded one.
All inputs are finite; a program needn't handle non-finite values. No bound on the sum of `key_keep` on one device may be relied on, other than what follows from the above.
Results may differ from a plain program's by a relative error of at most 0.0089.
Values may be sent and summed in bfloat16 or wider, within the bound.
A program may use at most 128 MiB of HBM per device.

v0:
```python
import jax
import jax.numpy as jnp
import numpy as np
from jax import lax
from jax.sharding import PartitionSpec as P

EPS_NORM = 1e-05
EPS_DIR = 1e-06


def with_halo(block, sides, width, periodic):
    for axis, dim in sides:
        count = lax.axis_size(axis)
        forward = [(i, i + 1) for i in range(count - 1)]
        if periodic:
            forward.append((count - 1, 0))
        backward = [(target, source) for source, target in forward]
        low = lax.ppermute(
            lax.slice_in_dim(block, block.shape[dim] - width, None, axis=dim), axis, forward
        )
        high = lax.ppermute(lax.slice_in_dim(block, 0, width, axis=dim), axis, backward)
        block = jnp.concatenate([low, block, high], axis=dim)
    return block


def normed(row_data, norm_gain):
    row_mean = jnp.mean(row_data, axis=-1, keepdims=True)
    centered = row_data - row_mean
    variance = jnp.mean(centered * centered, axis=-1, keepdims=True)
    return centered * lax.rsqrt(variance + EPS_NORM) * norm_gain


def unit_dir(vectors):
    return vectors * lax.rsqrt(jnp.sum(vectors * vectors, axis=-1, keepdims=True) + EPS_DIR)


def attend(query, keys, values, allowed, scale):
    num_heads = scale.shape[0]
    blocks, query_count, channels = query.shape
    key_count = keys.shape[1]
    head_size = channels // num_heads
    query_dir = unit_dir(query.reshape(blocks, query_count, num_heads, head_size))
    key_dir = unit_dir(keys.reshape(blocks, key_count, num_heads, head_size))
    value_heads = values.reshape(blocks, key_count, num_heads, head_size)
    cosine = jnp.einsum("bqhd,bkhd->bhqk", query_dir, key_dir, precision=lax.Precision.HIGHEST)
    scale_row = scale[None, :, None, None]
    numer = jnp.exp(scale_row * cosine - scale_row) * allowed[:, None, :, :]
    weights = numer / jnp.sum(numer, axis=-1, keepdims=True)
    result = jnp.einsum("bhqk,bkhd->bqhd", weights, value_heads, precision=lax.Precision.HIGHEST)
    return result.reshape(blocks, query_count, channels)


def contract(left, right, left_dim, right_dim):
    return lax.dot_general(
        left, right, (((left_dim,), (right_dim,)), ((), ())), preferred_element_type=jnp.float32
    )


def self_table(levels, blocks):
    table = np.zeros((blocks, levels * 36, levels * 72), np.float32)
    lev_idx, row_idx, col_idx = np.meshgrid(
        np.arange(levels), np.arange(3), np.arange(12), indexing="ij"
    )
    query_pos = (lev_idx * 36 + row_idx * 12 + col_idx).reshape(-1)
    for block_idx in range(blocks):
        offset = 3 * (1 - block_idx % 2)
        key_pos = (lev_idx * 72 + (row_idx + offset) * 12 + col_idx).reshape(-1)
        table[block_idx, query_pos, key_pos] = 1.0
    return table


def window_out(query, kv_ext, keep_ext, scale):
    levels, rows_n, cols_n, channels = query.shape
    blocks = rows_n // 3
    row_wins = rows_n // 6 + 1
    col_wins = cols_n // 12 + 1
    padded_q = jnp.pad(query, ((0, 0), (0, 0), (6, 6), (0, 0)))
    query_win = padded_q.reshape(levels, blocks, 3, col_wins, 12, channels).transpose(
        1, 3, 0, 2, 4, 5
    )
    query_win = query_win.reshape(blocks * col_wins, levels * 36, channels)
    pick = (np.arange(blocks) + 1) // 2
    kv_win = kv_ext.reshape(levels, row_wins, 6, col_wins, 12, 2 * channels).transpose(
        1, 3, 0, 2, 4, 5
    )[pick]
    kv_win = kv_win.reshape(blocks * col_wins, levels * 72, 2 * channels)
    keep_win = keep_ext.reshape(levels, row_wins, 6, col_wins, 12).transpose(1, 3, 0, 2, 4)[pick]
    keep_win = keep_win.reshape(blocks, col_wins, 1, levels * 72).astype(jnp.float32)
    table = jnp.asarray(self_table(levels, blocks)).astype(jnp.float32)
    allowed = jnp.maximum(keep_win, table[:, None]).reshape(
        blocks * col_wins, levels * 36, levels * 72
    )
    result = attend(query_win, kv_win[..., :channels], kv_win[..., channels:], allowed, scale)
    result = result.reshape(blocks, col_wins, levels, 3, 12, channels).transpose(2, 0, 3, 1, 4, 5)
    return result.reshape(levels, rows_n, cols_n + 12, channels)[:, :, 6:-6]


def extend_lon(payload):
    return with_halo(payload, (("lon", 2),), 6, True)


def extend_lat(payload):
    return with_halo(payload, (("lat", 1),), 3, False)


def marks_lon(marks):
    return with_halo(marks, (("lon", 2),), 6, True)


def marks_lat(marks):
    return with_halo(marks, (("lat", 1),), 3, False)


def extend(payload, marks):
    return (extend_lat(extend_lon(payload)), marks_lat(marks_lon(marks)))


def retract_lat(grads):
    rims = jnp.concatenate([grads[:, :3], grads[:, -3:]], axis=1)
    got = with_halo(rims.astype(jnp.bfloat16), (("lat", 1),), 3, False).astype(rims.dtype)
    inner = grads[:, 3:-3]
    return jnp.concatenate(
        [inner[:, :3] + got[:, :3], inner[:, 3:-3], inner[:, -3:] + got[:, -3:]], axis=1
    )


def retract_lon(grads):
    rims = jnp.concatenate([grads[:, :, :6], grads[:, :, -6:]], axis=2)
    got = with_halo(rims.astype(jnp.bfloat16), (("lon", 2),), 6, True).astype(rims.dtype)
    inner = grads[:, :, 6:-6]
    return jnp.concatenate(
        [inner[:, :, :6] + got[:, :, :6], inner[:, :, 6:-6], inner[:, :, -6:] + got[:, :, -6:]],
        axis=2,
    )


def retract(grads):
    return retract_lon(retract_lat(grads))


def per_device(tokens, cotangent, key_keep, norm_gain, w_qkv, w_proj, attn_scale):
    levels, rows_n, cols_n, channels = tokens.shape
    row_data = tokens.reshape(-1, channels).astype(jnp.float32)
    normal_y = normed(row_data, norm_gain).astype(jnp.bfloat16)
    keep_mark = key_keep.astype(jnp.bfloat16)
    qkv = jnp.dot(normal_y, w_qkv, preferred_element_type=jnp.float32).astype(jnp.bfloat16)
    query = qkv[:, :channels]
    kv_ext, keep_ext = extend(
        qkv[:, channels:].reshape(levels, rows_n, cols_n, 2 * channels), keep_mark
    )

    def attend_local(query_in, kv_in, scale_in):
        return window_out(query_in, kv_in, keep_ext, scale_in)

    query_grid = query.reshape(levels, rows_n, cols_n, channels).astype(jnp.float32)
    attended_f, pull = jax.vjp(attend_local, query_grid, kv_ext.astype(jnp.float32), attn_scale)
    attended = attended_f.reshape(-1, channels).astype(jnp.bfloat16)
    mixed = (row_data + jnp.dot(attended, w_proj, preferred_element_type=jnp.float32)).astype(
        jnp.bfloat16
    )
    g_rows = cotangent.reshape(-1, channels)
    part_proj = contract(attended, g_rows, 0, 0)
    d_att = contract(g_rows, w_proj, 1, 1).astype(jnp.bfloat16)
    d_query, d_kv_ext, d_scale = pull(
        d_att.reshape(levels, rows_n, cols_n, channels).astype(jnp.float32)
    )
    d_kv = retract(d_kv_ext)
    d_qkv = jnp.concatenate(
        [d_query.reshape(-1, channels), d_kv.reshape(-1, 2 * channels)], axis=1
    ).astype(jnp.bfloat16)
    part_qkv = contract(normal_y, d_qkv, 0, 0)
    d_normal = contract(d_qkv, w_qkv, 1, 1)
    pull_norm = jax.vjp(normed, row_data, norm_gain)[1]
    d_rows, d_gain = pull_norm(d_normal)
    grad_tokens = (g_rows.astype(jnp.float32) + d_rows).astype(jnp.bfloat16)
    grad_qkv, grad_proj, grad_gain, grad_scale = lax.psum(
        (part_qkv, part_proj, d_gain, d_scale), ("lat", "lon")
    )
    return (
        mixed.reshape(tokens.shape),
        grad_tokens.reshape(tokens.shape),
        grad_qkv,
        grad_proj,
        grad_gain,
        grad_scale,
    )


def solution(mesh):
    placed = (
        P(None, "lat", "lon", None),
        P(None, "lat", "lon", None),
        P(None, "lat", "lon"),
        P(),
        P(),
        P(),
        P(),
    )
    return jax.shard_map(
        per_device,
        mesh=mesh,
        in_specs=placed,
        out_specs=(P(None, "lat", "lon", None), P(None, "lat", "lon", None), P(), P(), P(), P()),
        check_vma=False,
    )
```

profile of v0, /device:TPU:1, one launch (start us, length us, event | category | flops | bytes accessed | tf_op | source)
XLA Modules:
  0.0 400.3 jit_solution(7561955838881486711)
XLA Ops:
  14.1 2.5 collective-permute-start
  17.4 5.3 %collective-permute-start.1 = (bf16[2,6,6,1024]{3,0,2,1:T(2,128)(2,1)}, bf16[2,6,6,1024]{3,0,2,1:T(2,128)(2,1)}, u32[]{:S(2)}, u32[]{:S(2)}) collective-permute-start(bf16[2,6,6,1024]{3,0,2,1:T(2,128)(2,1)} %copy.166), channel_id=1, source_target_pairs={{1,0},{2,1},{3,2},{4,3},{5,4},{6,5},{7,6},{8,7},{9,8},{10,9},{11,1... | collective-permute-start | bytes 442376 | tf_op jit(solution)/shard_map/ppermute | solution.py:21
  22.8 5.7 %collective-permute-start.5 = (bf16[2,6,6]{2,0,1:T(2,128)(2,1)S(1)}, bf16[2,6,6]{2,0,1:T(2,128)(2,1)S(1)}, u32[]{:S(2)}, u32[]{:S(2)}) collective-permute-start(bf16[2,6,6]{2,0,1:T(2,128)(2,1)S(1)} %get-tuple-element.30), channel_id=1, source_target_pairs={{1,0},{2,1},{3,2},{4,3},{5,4},{6,5},{7,6},{8,7},{9,8},{10,9},{11,1... | collective-permute-start | bytes 440 | tf_op jit(solution)/shard_map/ppermute | solution.py:21
  34.7 2.2 convolution_convert_fusion.1
  45.0 5.9 %collective-permute-start.2 = (bf16[2,3,36,1024]{3,0,2,1:T(2,128)(2,1)}, bf16[2,3,36,1024]{3,0,2,1:T(2,128)(2,1)}, u32[]{:S(2)}, u32[]{:S(2)}) collective-permute-start(bf16[2,3,36,1024]{3,0,2,1:T(2,128)(2,1)} %get-tuple-element.23), channel_id=1, source_target_pairs={{0,32},{32,64},{64,96},{1,33},{33,65},{65,97},{2,34},{34,66},{66,9... | collective-permute-start | bytes 1327112 | tf_op jit(solution)/shard_map/ppermute | solution.py:18
  51.0 1.9 collective-permute-start.3
  53.0 5.1 %collective-permute-start.6 = (bf16[2,3,36]{2,0,1:T(2,128)(2,1)S(1)}, bf16[2,3,36]{2,0,1:T(2,128)(2,1)S(1)}, u32[]{:S(2)}, u32[]{:S(2)}) collective-permute-start(bf16[2,3,36]{2,0,1:T(2,128)(2,1)S(1)} %get-tuple-element.27), channel_id=1, source_target_pairs={{0,32},{32,64},{64,96},{1,33},{33,65},{65,97},{2,34},{34,66},{66,9... | collective-permute-start | bytes 1304 | tf_op jit(solution)/shard_map/ppermute | solution.py:18
  61.6 2.5 reshape.233
  64.2 2.3 copy.150
  69.0 3.8 pad_maximum_fusion.1
  74.0 3.2 transpose.58
  77.3 6.7 %gather_fusion = bf16[2,3,2,6,12,1024]{5,2,4,1,3,0:T(2,128)(2,1)} fusion(bf16[2,3,2,6,12,1024]{5,2,4,1,3,0:T(2,128)(2,1)} %bitcast.93, s32[1024]{0:T(1024)S(1)} %pad_clamp_fusion), kind=kCustom, calls=%fused_computation | custom fusion | bytes 3538952 | tf_op jit(solution)/shard_map/jvp()/gather | solution.py:83
  84.0 7.9 %gather_fusion.1 = f32[2,3,2,6,12,1024]{5,2,4,1,3,0:T(2,128)} fusion(f32[2,3,2,6,12,1024]{5,2,4,1,3,0:T(2,128)} %transpose.58, s32[1024]{0:T(1024)S(1)} %pad_clamp_fusion), kind=kCustom, calls=%fused_computation.1 | custom fusion | bytes 7077896 | tf_op jit(solution)/shard_map/jvp()/gather | solution.py:83
  91.9 5.3 %copy.142 = f32[2,3,2,6,12,1024]{5,4,3,2,1,0:T(8,128)} copy(f32[2,3,2,6,12,1024]{5,2,4,1,3,0:T(2,128)} %gather_fusion.1) | data formatting | bytes 7077888 | tf_op jit(solution)/shard_map/jvp()/gather | solution.py:83
  97.1 5.2 %reshape.225 = f32[6,144,1024]{2,1,0:T(8,128)} reshape(f32[2,3,2,6,12,1024]{5,4,3,2,1,0:T(8,128)} %copy.142) | data formatting | bytes 7077888 | tf_op jit(solution)/shard_map/jvp()/reshape | solution.py:86
  102.3 2.9 slice.135
  105.3 3.3 copy.143
  108.6 2.5 multiply_reduce_fusion.2
  111.4 6.7 %multiply_reduce_fusion.3 = (f32[6,8,72]{2,1,0:T(8,128)S(1)}, f32[6,8,72,144]{3,2,1,0:T(8,128)}) fusion(f32[6,72,144]{2,1,0:T(8,128)} %broadcast_maximum_fusion, f32[8]{0:T(128)S(1)} %copy-done.26, f32[6,144,8,64]{1,3,2,0:T(8,128)S(1)} %bitcast.87, f32[6,144,8]{1,2,0:T(8,128)S(1)} %add_rsqrt_fusion, f32[6,72,8,64]{1,3,2,0:T(8,128)S(1)} %copy.141, ...), kind=kOutput, calls=%fused_computation.19 | convolution fusion | flops 384856704 | bytes 4949024 | tf_op jit(solution)/shard_map/jvp(bqhd,bkhd->bhqk)/dot_general | solution.py:45
  118.1 2.1 copy.136
  120.2 3.8 reshape.220
  124.0 2.1 slice.133
  126.2 2.5 copy.137
  128.7 6.8 %fusion.18 = f32[6,8,64,144]{3,2,1,0:T(8,128)} fusion(f32[6,8,72]{2,1,0:T(8,128)S(1)} %get-tuple-element.31, f32[6,72,144]{2,1,0:T(8,128)} %broadcast_maximum_fusion, bf16[6,72,8,64]{1,3,2,0:T(8,128)(2,1)} %copy.150, f32[6,8,72,144]{3,2,1,0:T(8,128)} %get-tuple-element.32, f32[8]{0:T(128)S(1)} %copy-done.26), kind=kOutput, calls=%fused_computation.48 | convolution fusion | flops 384196608 | bytes 4465184 | tf_op jit(solution)/shard_map/transpose(jvp(bhqk,bkhd->bqhd))/dot_general | solution.py:49
  135.5 2.1 multiply_reduce_fusion.1
  137.6 2.5 fusion.34
  140.1 4.0 %fusion.12 = (f32[6,72,8]{1,2,0:T(8,128)S(1)}, f32[6,8,72,64]{2,3,1,0:T(8,128)S(1)}) fusion(f32[6,72,8,64]{1,3,2,0:T(8,128)S(1)} %copy.141, f32[6,144,8,64]{1,3,2,0:T(8,128)S(1)} %bitcast.88, f32[6,144,8]{1,2,0:T(8,128)S(1)} %add_rsqrt_fusion, f32[6,8,72,144]{3,2,1,0:T(8,128)S(1)} %get-tuple-element.14, f32[8]{0:T(128)S(1)} %copy-done.26), kind=kOutput, calls=%fused_computation.38 | convolution fusion | flops 383584896 | bytes 5571104 | tf_op jit(solution)/shard_map/transpose(jvp(bqhd,bkhd->bhqk))/dot_general | solution.py:45
  144.2 6.0 %fusion.4 = (f32[6,144,8]{1,2,0:T(8,128)}, f32[6,8,144,64]{2,3,1,0:T(8,128)}) fusion(f32[6,144,512]{1,2,0:T(8,128)S(1)} %copy-done.2, f32[6,72,8,64]{1,3,2,0:T(8,128)S(1)} %copy.141, f32[6,72,8]{1,2,0:T(8,128)S(1)} %add_rsqrt_fusion.1, f32[6,8,72,144]{3,2,1,0:T(8,128)S(1)} %get-tuple-element.14, f32[8]{0:T(128)S(1)} %copy-done.26), kind=kOutput, calls=%fused_computation.16 | convolution fusion | flops 383802624 | bytes 6455840 | tf_op jit(solution)/shard_map/transpose(jvp(bqhd,bkhd->bhqk))/dot_general | solution.py:45
  155.1 2.3 copy.156
  157.5 5.7 %add_add_fusion = f32[6,144,8,64]{1,3,2,0:T(8,128)} fusion(f32[6,8,144,64]{2,3,1,0:T(8,128)} %get-tuple-element.36, f32[6,144,8]{1,2,0:T(8,128)S(1)} %multiply_multiply_fusion.1, f32[6,144,8]{1,2,0:T(8,128)S(1)} %add_rsqrt_fusion, f32[6,144,512]{1,2,0:T(8,128)} %copy.143), kind=kLoop, calls=%fused_computation.4 | loop fusion | flops 1769472 | bytes 5363712 | tf_op jit(solution)/shard_map/transpose(jvp())/add_any | solution.py:34
  163.2 3.2 copy.157
  166.4 3.6 pad_add_fusion
  170.1 4.9 %reshape.278 = f32[2,3,2,6,12,1024]{5,4,3,2,1,0:T(8,128)} reshape(f32[6,144,1024]{2,1,0:T(8,128)} %pad_add_fusion) | data formatting | bytes 7077888 | tf_op jit(solution)/shard_map/transpose(jvp())/reshape | solution.py:86
  175.0 7.1 %copy.158 = f32[2,3,2,6,12,1024]{5,2,4,3,1,0:T(2,128)} copy(f32[2,3,2,6,12,1024]{5,4,3,2,1,0:T(8,128)} %reshape.278) | data formatting | bytes 7077888 | tf_op jit(solution)/shard_map/transpose(jvp())/reshape | solution.py:86
  182.1 3.4 broadcast_in_dim.43
  185.5 8.8 %scatter_fusion = f32[2,3,2,6,12,1024]{5,2,4,3,1,0:T(2,128)} fusion(f32[2,3,2,6,12,1024]{5,2,4,3,1,0:T(2,128)} %broadcast_in_dim.43, s32[2]{0:T(128)S(1)} %iota.5, f32[2,3,2,6,12,1024]{5,2,4,3,1,0:T(2,128)} %copy.158), kind=kCustom, calls=%fused_computation.3 | custom fusion | flops 884736 | bytes 10616840 | tf_op jit(solution)/shard_map/transpose(jvp())/scatter-add | solution.py:83
  194.3 3.4 copy.159
  200.6 5.3 %collective-permute-start.8 = (bf16[2,3,36,1024]{3,0,2,1:T(2,128)(2,1)S(1)}, bf16[2,3,36,1024]{3,0,2,1:T(2,128)(2,1)}, u32[]{:S(2)}, u32[]{:S(2)}) collective-permute-start(bf16[2,3,36,1024]{3,0,2,1:T(2,128)(2,1)S(1)} %get-tuple-element.19), channel_id=1, source_target_pairs={{0,32},{32,64},{64,96},{1,33},{33,65},{65,97},{2,34},{34,66},{66,9... | collective-permute-start | bytes 1327112 | tf_op jit(solution)/shard_map/ppermute | solution.py:18
  205.8 1.9 collective-permute-start.9
  207.8 4.0 convolution_bitcast_fusion
  214.6 2.6 collective-permute-done.9
  217.3 2.7 convert_add_fusion
  221.3 5.7 %collective-permute-start.11 = (bf16[2,6,6,1024]{3,0,2,1:T(2,128)(2,1)S(1)}, bf16[2,6,6,1024]{3,0,2,1:T(2,128)(2,1)S(1)}, u32[]{:S(2)}, u32[]{:S(2)}) collective-permute-start(bf16[2,6,6,1024]{3,0,2,1:T(2,128)(2,1)S(1)} %get-tuple-element.22), channel_id=1, source_target_pairs={{1,0},{2,1},{3,2},{4,3},{5,4},{6,5},{7,6},{8,7},{9,8},{10,9},{11,1... | collective-permute-start | bytes 442376 | tf_op jit(solution)/shard_map/ppermute | solution.py:21
  230.9 2.8 fusion.24
  234.8 2.1 fusion.17
  238.1 65.9 %all-reduce.4 = (f32[512]{0:T(512)}, f32[8]{0:T(128)}) all-reduce(f32[512]{0:T(512)S(1)} %get-tuple-element.8, f32[8]{0:T(128)S(1)} %negate_add_fusion), channel_id=1, replica_groups=mesh['lat'=4,'lon'=32] {'lat','lon'}, use_global_device_ids=true, to_apply=%region_14.15 | all-reduce | flops 520 | bytes 4160 | tf_op jit(solution)/shard_map/psum | solution.py:176
  305.8 82.4 %all-reduce.8.cloned.1.call-done = (f32[512,1536]{1,0:T(8,128)}, f32[512,512]{1,0:T(8,128)}) async-done(((f32[512,1536]{1,0:T(8,128)}, f32[512,512]{1,0:T(8,128)}), (f32[512,1536]{1,0:T(8,128)}, f32[512,512]{1,0:T(8,128)})) %all-reduce.8.cloned.1.call-update) | async-done | bytes 4194320 | tf_op jit(solution)/shard_map/psum | solution.py:176
  388.2 3.8 copy.175
  (148 shorter events, 50.5 us)
Async XLA Ops:
  7.2 3.7 copy-start
  7.2 381.0 %all-reduce.8.cloned.1.call-start = ((), (), s32[]{:S(2)}) async-start(), calls=%async_computation | async-start | bytes 8388608 | tf_op jit(solution)/shard_map/psum | solution.py:176
  10.8 2.5 copy-start.16
  10.9 11.8 %copy-start.27 = (s32[2,6,24]{2,0,1:T(2,128)S(1)}, s32[2,6,24]{2,0,1:T(2,128)}, u32[]{:S(2)}) copy-start(s32[2,6,24]{2,0,1:T(2,128)} %param.13) | copy-start | bytes 3460
  12.4 0.8 copy-start.14
  14.1 24.7 %collective-permute-start = (bf16[2,6,6,1024]{3,0,2,1:T(2,128)(2,1)}, bf16[2,6,6,1024]{3,0,2,1:T(2,128)(2,1)}, u32[]{:S(2)}, u32[]{:S(2)}) collective-permute-start(bf16[2,6,6,1024]{3,0,2,1:T(2,128)(2,1)} %copy.165), channel_id=1, source_target_pairs={{0,1},{1,2},{2,3},{3,4},{4,5},{5,6},{6,7},{7,8},{8,9},{9,10},{10,1... | collective-permute-start | bytes 442376 | tf_op jit(solution)/shard_map/ppermute | solution.py:18
  17.4 24.2 %collective-permute-start.1 = (bf16[2,6,6,1024]{3,0,2,1:T(2,128)(2,1)}, bf16[2,6,6,1024]{3,0,2,1:T(2,128)(2,1)}, u32[]{:S(2)}, u32[]{:S(2)}) collective-permute-start(bf16[2,6,6,1024]{3,0,2,1:T(2,128)(2,1)} %copy.166), channel_id=1, source_target_pairs={{1,0},{2,1},{3,2},{4,3},{5,4},{6,5},{7,6},{8,7},{9,8},{10,9},{11,1... | collective-permute-start | bytes 442376 | tf_op jit(solution)/shard_map/ppermute | solution.py:21
  22.8 30.1 %collective-permute-start.4 = (bf16[2,6,6]{2,0,1:T(2,128)(2,1)S(1)}, bf16[2,6,6]{2,0,1:T(2,128)(2,1)S(1)}, u32[]{:S(2)}, u32[]{:S(2)}) collective-permute-start(bf16[2,6,6]{2,0,1:T(2,128)(2,1)S(1)} %get-tuple-element.29), channel_id=1, source_target_pairs={{0,1},{1,2},{2,3},{3,4},{4,5},{5,6},{6,7},{7,8},{8,9},{9,10},{10,1... | collective-permute-start | bytes 440 | tf_op jit(solution)/shard_map/ppermute | solution.py:18
  22.8 30.1 %collective-permute-start.5 = (bf16[2,6,6]{2,0,1:T(2,128)(2,1)S(1)}, bf16[2,6,6]{2,0,1:T(2,128)(2,1)S(1)}, u32[]{:S(2)}, u32[]{:S(2)}) collective-permute-start(bf16[2,6,6]{2,0,1:T(2,128)(2,1)S(1)} %get-tuple-element.30), channel_id=1, source_target_pairs={{1,0},{2,1},{3,2},{4,3},{5,4},{6,5},{7,6},{8,7},{9,8},{10,9},{11,1... | collective-permute-start | bytes 440 | tf_op jit(solution)/shard_map/ppermute | solution.py:21
  32.4 4.5 %copy-start.7 = (f32[6,72,8,64]{3,2,1,0:T(8,128)}, f32[6,72,8,64]{3,2,1,0:T(8,128)S(1)}, u32[]{:S(2)}) copy-start(f32[6,72,8,64]{3,2,1,0:T(8,128)S(1)} %reshape.245) | copy-start | bytes 2654212
  37.0 23.1 %copy-start.21 = (bf16[288,512]{1,0:T(8,128)(2,1)S(1)}, bf16[288,512]{1,0:T(8,128)(2,1)}, u32[]{:S(2)}) copy-start(bf16[288,512]{1,0:T(8,128)(2,1)} %convolution_convert_fusion.1) | copy-start | bytes 884740
  42.6 0.9 copy-start.15
  45.0 24.0 %collective-permute-start.2 = (bf16[2,3,36,1024]{3,0,2,1:T(2,128)(2,1)}, bf16[2,3,36,1024]{3,0,2,1:T(2,128)(2,1)}, u32[]{:S(2)}, u32[]{:S(2)}) collective-permute-start(bf16[2,3,36,1024]{3,0,2,1:T(2,128)(2,1)} %get-tuple-element.23), channel_id=1, source_target_pairs={{0,32},{32,64},{64,96},{1,33},{33,65},{65,97},{2,34},{34,66},{66,9... | collective-permute-start | bytes 1327112 | tf_op jit(solution)/shard_map/ppermute | solution.py:18
  51.0 18.0 %collective-permute-start.3 = (bf16[2,3,36,1024]{3,0,2,1:T(2,128)(2,1)}, bf16[2,3,36,1024]{3,0,2,1:T(2,128)(2,1)}, u32[]{:S(2)}, u32[]{:S(2)}) collective-permute-start(bf16[2,3,36,1024]{3,0,2,1:T(2,128)(2,1)} %get-tuple-element.24), channel_id=1, source_target_pairs={{32,0},{64,32},{96,64},{33,1},{65,33},{97,65},{34,2},{66,34},{98,6... | collective-permute-start | bytes 1327112 | tf_op jit(solution)/shard_map/ppermute | solution.py:21
  53.0 13.4 %collective-permute-start.6 = (bf16[2,3,36]{2,0,1:T(2,128)(2,1)S(1)}, bf16[2,3,36]{2,0,1:T(2,128)(2,1)S(1)}, u32[]{:S(2)}, u32[]{:S(2)}) collective-permute-start(bf16[2,3,36]{2,0,1:T(2,128)(2,1)S(1)} %get-tuple-element.27), channel_id=1, source_target_pairs={{0,32},{32,64},{64,96},{1,33},{33,65},{65,97},{2,34},{34,66},{66,9... | collective-permute-start | bytes 1304 | tf_op jit(solution)/shard_map/ppermute | solution.py:18
  58.2 8.3 %collective-permute-start.7 = (bf16[2,3,36]{2,0,1:T(2,128)(2,1)S(1)}, bf16[2,3,36]{2,0,1:T(2,128)(2,1)S(1)}, u32[]{:S(2)}, u32[]{:S(2)}) collective-permute-start(bf16[2,3,36]{2,0,1:T(2,128)(2,1)S(1)} %get-tuple-element.28), channel_id=1, source_target_pairs={{32,0},{64,32},{96,64},{33,1},{65,33},{97,65},{34,2},{66,34},{98,6... | collective-permute-start | bytes 1304 | tf_op jit(solution)/shard_map/ppermute | solution.py:21
  72.8 1.2 copy-start.6
  105.3 5.8 %copy-start.26 = (f32[8]{0:T(128)S(1)}, f32[8]{0:T(128)}, u32[]{:S(2)}) copy-start(f32[8]{0:T(128)} %param.17) | copy-start | bytes 100
  108.6 2.8 copy-start.1
  111.4 6.7 %copy-start.8 = (bf16[2,3,2,6,12,1024]{5,2,4,1,3,0:T(2,128)(2,1)S(1)}, bf16[2,3,2,6,12,1024]{5,2,4,1,3,0:T(2,128)(2,1)}, u32[]{:S(2)}) copy-start(bf16[2,3,2,6,12,1024]{5,2,4,1,3,0:T(2,128)(2,1)} %gather_fusion) | copy-start | bytes 5308420
  128.7 6.8 %copy-start.3 = (f32[6,8,72,144]{3,2,1,0:T(8,128)S(1)}, f32[6,8,72,144]{3,2,1,0:T(8,128)}, u32[]{:S(2)}) copy-start(f32[6,8,72,144]{3,2,1,0:T(8,128)} %get-tuple-element.32) | copy-start | bytes 5971972
  128.7 6.8 %copy-start.10 = (f32[6,72,144]{2,1,0:T(8,128)S(1)}, f32[6,72,144]{2,1,0:T(8,128)}, u32[]{:S(2)}) copy-start(f32[6,72,144]{2,1,0:T(8,128)} %broadcast_maximum_fusion) | copy-start | bytes 746500
  128.7 6.8 %copy-start.12 = (bf16[6,144,512]{1,2,0:T(8,128)(2,1)S(1)}, bf16[6,144,512]{1,2,0:T(8,128)(2,1)}, u32[]{:S(2)}) copy-start(bf16[6,144,512]{1,2,0:T(8,128)(2,1)} %copy.137) | copy-start | bytes 2654212
  128.7 6.8 %copy-start.18 = (bf16[6,72,8,64]{1,3,2,0:T(8,128)(2,1)S(1)}, bf16[6,72,8,64]{1,3,2,0:T(8,128)(2,1)}, u32[]{:S(2)}) copy-start(bf16[6,72,8,64]{1,3,2,0:T(8,128)(2,1)} %copy.150) | copy-start | bytes 1327108
  137.6 2.5 copy-start.2
  154.2 3.3 copy-start.24
  197.7 2.9 copy-start.5
  197.7 10.1 %copy-start.4 = (f32[6,8,72,144]{3,2,1,0:T(8,128)S(1)}, f32[6,8,72,144]{3,2,1,0:T(8,128)}, u32[]{:S(2)}) copy-start(f32[6,8,72,144]{3,2,1,0:T(8,128)} %get-tuple-element.32) | copy-start | bytes 5971972
  197.7 10.1 %copy-start.11 = (f32[6,72,144]{2,1,0:T(8,128)S(1)}, f32[6,72,144]{2,1,0:T(8,128)}, u32[]{:S(2)}) copy-start(f32[6,72,144]{2,1,0:T(8,128)} %broadcast_maximum_fusion) | copy-start | bytes 746500
  197.7 10.1 %copy-start.13 = (bf16[6,144,512]{1,2,0:T(8,128)(2,1)S(1)}, bf16[6,144,512]{1,2,0:T(8,128)(2,1)}, u32[]{:S(2)}) copy-start(bf16[6,144,512]{1,2,0:T(8,128)(2,1)} %copy.137) | copy-start | bytes 2654212
  200.6 14.1 %collective-permute-start.8 = (bf16[2,3,36,1024]{3,0,2,1:T(2,128)(2,1)S(1)}, bf16[2,3,36,1024]{3,0,2,1:T(2,128)(2,1)}, u32[]{:S(2)}, u32[]{:S(2)}) collective-permute-start(bf16[2,3,36,1024]{3,0,2,1:T(2,128)(2,1)S(1)} %get-tuple-element.19), channel_id=1, source_target_pairs={{0,32},{32,64},{64,96},{1,33},{33,65},{65,97},{2,34},{34,66},{66,9... | collective-permute-start | bytes 1327112 | tf_op jit(solution)/shard_map/ppermute | solution.py:18
  205.8 11.4 %collective-permute-start.9 = (bf16[2,3,36,1024]{3,0,2,1:T(2,128)(2,1)}, bf16[2,3,36,1024]{3,0,2,1:T(2,128)(2,1)}, u32[]{:S(2)}, u32[]{:S(2)}) collective-permute-start(bf16[2,3,36,1024]{3,0,2,1:T(2,128)(2,1)} %get-tuple-element.20), channel_id=1, source_target_pairs={{32,0},{64,32},{96,64},{33,1},{65,33},{97,65},{34,2},{66,34},{98,6... | collective-permute-start | bytes 1327112 | tf_op jit(solution)/shard_map/ppermute | solution.py:21
  214.6 12.3 %copy-start.20 = (bf16[2,6,24,512]{3,0,2,1:T(2,128)(2,1)}, bf16[2,6,24,512]{3,0,2,1:T(2,128)(2,1)S(1)}, u32[]{:S(2)}) copy-start(bf16[2,6,24,512]{3,0,2,1:T(2,128)(2,1)S(1)} %slice.140) | copy-start | bytes 884740
  214.6 12.3 %copy-start.22 = (bf16[2,6,24,512]{3,2,1,0:T(8,128)(2,1)S(1)}, bf16[2,6,24,512]{3,2,1,0:T(8,128)(2,1)}, u32[]{:S(2)}) copy-start(bf16[2,6,24,512]{3,2,1,0:T(8,128)(2,1)} %param.12) | copy-start | bytes 884740
  221.2 8.3 %collective-permute-start.10 = (bf16[2,6,6,1024]{3,0,2,1:T(2,128)(2,1)S(1)}, bf16[2,6,6,1024]{3,0,2,1:T(2,128)(2,1)S(1)}, u32[]{:S(2)}, u32[]{:S(2)}) collective-permute-start(bf16[2,6,6,1024]{3,0,2,1:T(2,128)(2,1)S(1)} %get-tuple-element.21), channel_id=1, source_target_pairs={{0,1},{1,2},{2,3},{3,4},{4,5},{5,6},{6,7},{7,8},{8,9},{9,10},{10,1... | collective-permute-start | bytes 442376 | tf_op jit(solution)/shard_map/ppermute | solution.py:18
  221.3 8.2 %collective-permute-start.11 = (bf16[2,6,6,1024]{3,0,2,1:T(2,128)(2,1)S(1)}, bf16[2,6,6,1024]{3,0,2,1:T(2,128)(2,1)S(1)}, u32[]{:S(2)}, u32[]{:S(2)}) collective-permute-start(bf16[2,6,6,1024]{3,0,2,1:T(2,128)(2,1)S(1)} %get-tuple-element.22), channel_id=1, source_target_pairs={{1,0},{2,1},{3,2},{4,3},{5,4},{6,5},{7,6},{8,7},{9,8},{10,9},{11,1... | collective-permute-start | bytes 442376 | tf_op jit(solution)/shard_map/ppermute | solution.py:21
  228.4 2.5 copy-start.17
  228.4 2.5 copy-start.19
  228.4 2.5 copy-start.25
  233.7 1.1 copy-start.9
  388.2 3.8 copy-start.23
Sparse Core Ops, SparseCore 0:
  233.8 154.3 all-reduce.7
where the time goes:
time: 408 us; the launch traced here: 400 us
  local copies, waits for them, and re-layouts  104 us (25%)
  waiting for transfers between devices  86 us (21%)
  blocking collectives  65.9 us (16%)
  other arithmetic  47.3 us (12%)
  starting transfers between devices  41.4 us (10%)
  matrix products  40.2 us (10%)
  between operations  15.2 us (4%)
    psum x1, waiting for transfers between devices, per_device(): lax.psum((part_qkv, part_proj, d_gain, d_scale), ('lat', 'lon'))  82.4 us
    psum x1, blocking collectives, per_device(): lax.psum((part_qkv, part_proj, d_gain, d_scale), ('lat', 'lon'))  65.9 us
    ppermute x6, starting transfers between devices, with_halo(): lax.ppermute(lax.slice_in_dim(block, 0, width, axis=dim), axis, backward)  22.4 us
    gather x4, local copies, waits for them, and re-layouts, window_out(): kv_ext.reshape(levels, row_wins, 6, col_wins, 12, 2 * channels)  21.9 us
    reshape x4, local copies, waits for them, and re-layouts, window_out(): kv_win = kv_win.reshape(blocks * col_wins, levels * 72, 2 * channels)  21 us
    ppermute x6, starting transfers between devices, with_halo(): lax.ppermute(lax.slice_in_dim(block, block.shape[dim] - width, None, axis...  18.9 us
    dot_general x3, matrix products, attend(): jnp.einsum('bqhd,bkhd->bhqk', query_dir, key_dir, precision=lax.Precision...  16.7 us
    unnamed x63, local copies, waits for them, and re-layouts  13.6 us
  transfers between devices with their start and end apart: 13, of which 3 were waited for; matrix products, arithmetic and copies ran while one was open for 10% of the time, Pallas kernels for 0%

commit v1 on v0

v1 whole, which is shorter than its diff:
```python
import functools

import jax
import jax.numpy as jnp
import numpy as np
from jax import lax
from jax.experimental import pallas as pl
from jax.experimental.pallas import tpu as pltpu
from jax.sharding import PartitionSpec as P

EPS_NORM = 1e-05
EPS_DIR = 1e-06
MESH = pl.DeviceIdType.MESH
BF = jnp.bfloat16
F32 = jnp.float32

QUARTERS = ((1, 1), (1, 2), (0, 1), (0, 2), (1, 3), (1, 0), (0, 3), (0, 0))
QT = 40
ROWS = 80
WIN = 160
FLAG_ROW = 36


def token_of(quarter, t):
    half, cq = QUARTERS[quarter]
    lev, rest = divmod(t, 18)
    rr, cc = divmod(rest, 6)
    return lev * 144 + (half * 3 + rr) * 24 + cq * 6 + cc


def tables():
    perm = np.zeros((8 * QT, 288), np.float32)
    member = np.zeros((8, 288), np.float32)
    place = np.zeros((288, 256), np.float32)
    for quarter in range(8):
        for t in range(36):
            src = token_of(quarter, t)
            perm[quarter * QT + t, src] = 1.0
            member[quarter, src] = 1.0
            place[src, QT * (quarter % 4) + t] = 1.0
    return perm, member, place


def dot(a, b, ca=1, cb=0):
    return lax.dot_general(a, b, (((ca,), (cb,)), ((), ())), preferred_element_type=F32)


def position():
    lat = lax.axis_index("lat")
    lon = lax.axis_index("lon")
    return lat, lon


def wrap(value, count):
    return lax.rem(value + count, count)


SLOT_SENDS = ((2, "lat"), (5, "lon"), (7, "diag"), (6, "lat"), (3, "lat"))
KEPT_SLOTS = (0, 1, 4)

GROUPS = (
    (0, 768, "xzy"),
    (768, 512, "yxz"),
    (1280, 768, "zyx"),
    (2048, 768, "xzy"),
    (2816, 512, "yxz"),
    (3328, 768, "zyx"),
)


def slot_pieces(slot):
    if slot < 4:
        first = 2 * (slot // 2)
        kind = "xg"[slot % 2]
        return ((kind, first), (kind, first + 1))
    return (("x", slot), ("g", slot))


def coordinates():
    lat, lon = position()
    core = lax.rem(lat, 2)
    y = (lat // 2) * 2 + lon // 16
    x = lax.rem(lon // 4, 4)
    z = lax.rem(lon, 4)
    return {"x": x, "y": y, "z": z, "core": core}


def device_at(co):
    return ((co["y"] // 2) * 2 + co["core"], lax.rem(co["y"], 2) * 16 + co["x"] * 4 + co["z"])


def peer(co, axis, j):
    moved = dict(co)
    moved[axis] = lax.rem(co[axis] + j, 4)
    return device_at(moved)


def sibling(co):
    moved = dict(co)
    moved["core"] = 1 - co["core"]
    return device_at(moved)


def shift_in_kernel(
    x_hbm, g_hbm, keep_hbm, perm_hbm, member_hbm, place_hbm, wqkv_hbm, wproj_hbm, gain_hbm,
    win_ref, wqkv_ref, wproj_ref, gain_ref,
    x_ref, g_ref, keep_ref, perm_ref, member_ref, place_ref, in_buf, w_sem, in_send, in_recv,
):
    lat, lon = position()
    lat_lo, lat_hi = wrap(lat - 1, 4), wrap(lat + 1, 4)
    lon_lo, lon_hi = wrap(lon - 1, 32), wrap(lon + 1, 32)
    barrier = pltpu.get_barrier_semaphore()
    for dev in ((lat_hi, lon), (lat, lon_hi), (lat_hi, lon_hi)):
        pl.semaphore_signal(barrier, inc=1, device_id=dev, device_id_type=MESH)
    loads = []
    for i, (src, dst) in enumerate((
        (perm_hbm, perm_ref),
        (x_hbm, x_ref),
        (keep_hbm, keep_ref),
        (member_hbm, member_ref),
        (place_hbm, place_ref),
        (g_hbm, g_ref),
        (wqkv_hbm, wqkv_ref),
        (wproj_hbm, wproj_ref),
        (gain_hbm, gain_ref),
    )):
        loads.append(pltpu.make_async_copy(src, dst, w_sem.at[i]))
        loads[-1].start()
    for load in loads[:6]:
        load.wait()
    perm = perm_ref[...]
    xs = dot(perm, x_ref[...])
    gs = dot(perm, g_ref[...])
    keep_rows = [keep_ref[row, lev : lev + 1, :].astype(F32) for lev in range(2) for row in range(6)]
    marks = (jnp.concatenate(keep_rows, axis=1) * member_ref[...].astype(F32)).astype(BF)
    flags = dot(marks, place_ref[...])
    row_id = lax.broadcasted_iota(jnp.int32, (QT, 512), 0)

    def piece(kind, quarter):
        rows = slice(quarter * QT, (quarter + 1) * QT)
        if kind == "g":
            return gs[rows]
        flag = jnp.concatenate([flags[quarter : quarter + 1], jnp.zeros((1, 256), F32)], axis=1)
        return jnp.where(row_id == FLAG_ROW, flag, xs[rows])

    def payload(slot):
        return jnp.concatenate([piece(*p) for p in slot_pieces(slot)], axis=0).astype(BF)

    for i, (slot, _) in enumerate(SLOT_SENDS):
        in_buf[i] = payload(slot)
    pl.semaphore_wait(barrier, 3)
    low = {"lat": (lat_lo, lon), "lon": (lat, lon_lo), "diag": (lat_lo, lon_lo)}
    copies = []
    for i, (slot, way) in enumerate(SLOT_SENDS):
        copy = pltpu.make_async_remote_copy(
            src_ref=in_buf.at[i],
            dst_ref=win_ref.at[slot],
            send_sem=in_send.at[i],
            recv_sem=in_recv.at[i],
            device_id=low[way],
            device_id_type=MESH,
        )
        copy.start()
        copies.append(copy)
    for slot in KEPT_SLOTS:
        win_ref[slot] = payload(slot)
    for load in loads[6:]:
        load.wait()
    for copy in copies:
        copy.wait()


def block_sum_matrix():
    r = lax.broadcasted_iota(jnp.int32, (512, 512), 0)
    c = lax.broadcasted_iota(jnp.int32, (512, 512), 1)
    return jnp.where((r // 64) == (c // 64), 1.0, 0.0).astype(BF)


def head_sum(values, ones):
    hi = values.astype(BF)
    lo = (values - hi.astype(F32)).astype(BF)
    return dot(hi, ones) + dot(lo, ones)


def compute_kernel(
    win_ref, wqkv_ref, wproj_ref, gain_ref, scale_hbm,
    back_ref, grads_ref, small_ref,
    scale_ref, scale_sem, qd_s, kd_s, v_s, do_s, dq_s, dk_s, dv_s, att_s, allow_s, gs_s,
):
    scale_load = pltpu.make_async_copy(scale_hbm, scale_ref, scale_sem)
    scale_load.start()
    lat = lax.axis_index("lat")
    gain = gain_ref[...]
    slots = [win_ref[slot].astype(F32) for slot in range(8)]
    data = jnp.concatenate([slots[0], slots[2]] + [slots[slot][:QT] for slot in (4, 5, 6, 7)], axis=0)
    data = data.reshape(8, QT, 512)
    row_q = lax.broadcasted_iota(jnp.int32, (QT, 512), 0)
    x = jnp.where((row_q < 36)[None], data, 0.0).reshape(8 * QT, 512)
    g = jnp.concatenate([slots[1], slots[3]] + [slots[slot][QT:] for slot in (4, 5, 6, 7)], axis=0)
    g_b = g.astype(BF)
    mean = jnp.mean(x, axis=-1, keepdims=True)
    xc = x - mean
    var = jnp.mean(xc * xc, axis=-1, keepdims=True)
    rstd = lax.rsqrt(var + EPS_NORM)
    xhat = xc * rstd
    y = (xhat * gain).astype(BF)

    ones = block_sum_matrix()
    q = dot(y, wqkv_ref[:, 0:512]).astype(BF).astype(F32)
    k = dot(y, wqkv_ref[:, 512:1024]).astype(BF).astype(F32)
    v_s[...] = dot(y, wqkv_ref[:, 1024:1536]).astype(BF)
    rq = lax.rsqrt(head_sum(q * q, ones) + EPS_DIR)
    rk = lax.rsqrt(head_sum(k * k, ones) + EPS_DIR)
    qd = q * rq
    kd = k * rk
    qd_s[...] = qd.astype(BF)
    kd_s[...] = kd.astype(BF)
    do_s[...] = dot(g_b, wproj_ref[...], 1, 1).astype(BF)

    key_id = lax.broadcasted_iota(jnp.int32, (WIN, WIN), 0)
    query_id = lax.broadcasted_iota(jnp.int32, (WIN, WIN), 1)
    same_half = (key_id >= 2 * QT) == (query_id >= 2 * QT)
    joined = jnp.logical_or(same_half, lat != 3)
    first_row = lax.broadcasted_iota(jnp.int32, (8, WIN), 0) == 0
    one_row = jnp.where(first_row, 1.0, 0.0).astype(BF)
    for w in range(2):
        marks = data[4 * w, FLAG_ROW : FLAG_ROW + 1, :]
        for i in range(1, 4):
            marks = marks + data[4 * w + i, FLAG_ROW : FLAG_ROW + 1, :]
        marks = jnp.where(first_row, marks[:, :WIN], 0.0).astype(BF)
        keep = dot(marks, one_row, 0, 0)
        keep = jnp.where(joined, keep, 0.0)
        allow_s[w] = jnp.where(key_id == query_id, 1.0, keep)

    lane = lax.broadcasted_iota(jnp.int32, (1, 128), 1)
    scale_load.wait()

    def pair_window(pair, w):
        step = w * 4 + pair
        rows = slice(w * WIN, (w + 1) * WIN)
        cols = pl.ds(pl.multiple_of(pair * 128, 128), 128)
        qd_p = qd_s[rows, cols]
        kd_p = kd_s[rows, cols]
        v_p = v_s[rows, cols]
        do_p = do_s[rows, cols]
        allow = allow_s[w]
        acc_o = jnp.zeros((WIN, 128), F32)
        acc_q = jnp.zeros((WIN, 128), F32)
        acc_k = jnp.zeros((WIN, 128), F32)
        acc_v = jnp.zeros((WIN, 128), F32)
        zero = jnp.zeros((WIN, 128), BF)
        scales = [scale_ref[pair * 2 + i] for i in range(2)]
        for i in range(2):
            s = scales[i]
            mine = jnp.broadcast_to((lane < 64) if i == 0 else (lane >= 64), (WIN, 128))
            qd_h = jnp.where(mine, qd_p, zero)
            kd_h = jnp.where(mine, kd_p, zero)
            v_h = jnp.where(mine, v_p, zero)
            do_h = jnp.where(mine, do_p, zero)
            cos = dot(kd_p, qd_h, 1, 1)
            e = jnp.exp(s * cos - s) * allow
            p = e * (1.0 / jnp.sum(e, axis=0, keepdims=True))
            dp = dot(v_p, do_h, 1, 1)
            dl = p * (dp - jnp.sum(p * dp, axis=0, keepdims=True))
            gs_s[step, i : i + 1, :] = jnp.sum(dl * cos, axis=0, keepdims=True)
            p_b = p.astype(BF)
            dl_b = dl.astype(BF)
            acc_o = acc_o + dot(p_b, v_h, 0, 0)
            acc_v = acc_v + dot(p_b, do_h)
            acc_k = acc_k + dot(dl_b, qd_h)
            acc_q = acc_q + dot(dl_b, kd_h, 0, 0)
        s_lane = jnp.where(lane < 64, scales[0], scales[1])
        att_s[rows, cols] = acc_o.astype(BF)
        dv_s[rows, cols] = acc_v.astype(BF)
        dk_s[rows, cols] = acc_k * s_lane
        dq_s[rows, cols] = acc_q * s_lane

    def pair_step(pair, carry):
        pair_window(pair, 0)
        pair_window(pair, 1)
        return carry

    lax.fori_loop(0, 4, pair_step, 0)

    att = att_s[...]
    mixed = x + dot(att, wproj_ref[...])

    def put(block, value):
        for half in range(2):
            for ct in range(4):
                first = block * 1024 + ct * 256
                tile = value[half * 256 : (half + 1) * 256, ct * 128 : (ct + 1) * 128]
                grads_ref[half, first : first + 256] = tile.astype(BF)

    put(3, dot(att, g_b, 0, 0))
    dqd = dq_s[...]
    dq = (rq * (dqd - qd * head_sum(qd * dqd, ones))).astype(BF)
    dkd = dk_s[...]
    dk = (rk * (dkd - kd * head_sum(kd * dkd, ones))).astype(BF)
    dv = dv_s[...]
    put(2, dot(y, dv, 0, 0))
    put(1, dot(y, dk, 0, 0))
    put(0, dot(y, dq, 0, 0))
    dn = dot(dq, wqkv_ref[:, 0:512], 1, 1)
    dn = dn + dot(dk, wqkv_ref[:, 512:1024], 1, 1)
    dn = dn + dot(dv, wqkv_ref[:, 1024:1536], 1, 1)
    d_gain = jnp.sum(dn * xhat, axis=0, keepdims=True)
    dxh = dn * gain
    dx = rstd * (dxh - jnp.mean(dxh, axis=-1, keepdims=True) - xhat * jnp.mean(dxh * xhat, axis=-1, keepdims=True))
    gtok = g + dx
    for slot in (0, 2):
        rows = slice(slot * QT, (slot + 2) * QT)
        back_ref[slot] = mixed[rows].astype(BF)
        back_ref[slot + 1] = gtok[rows].astype(BF)
    for slot in (4, 5, 6, 7):
        rows = slice(slot * QT, (slot + 1) * QT)
        back_ref[slot] = jnp.concatenate([mixed[rows], gtok[rows]], axis=0).astype(BF)

    small_ref[...] = jnp.zeros((16, 128), F32)
    for i in range(4):
        small_ref[i : i + 1, :] = d_gain[:, i * 128 : (i + 1) * 128]
    for h in range(8):
        row = gs_s[h // 2, h % 2 : h % 2 + 1, :] + gs_s[4 + h // 2, h % 2 : h % 2 + 1, :]
        small_ref[8 + h : 9 + h, :] = jnp.broadcast_to(jnp.sum(row, axis=1, keepdims=True), (1, 128))


def reduce_kernel(
    back_ref, grads_ref, small_ref,
    ret_ref, sum_ref, small_out_ref,
    r0, a1, r1, a2, r2, a3, sv0, sv1, sv2, sv3,
    out_send, out_recv, sib_send, sib_recv, st_send, st_recv, sv_send, sv_recv,
):
    lat, lon = position()
    lat_lo, lat_hi = wrap(lat - 1, 4), wrap(lat + 1, 4)
    lon_lo, lon_hi = wrap(lon - 1, 32), wrap(lon + 1, 32)
    co = coordinates()
    core = co["core"]
    sib = sibling(co)
    peers = {axis: [peer(co, axis, j) for j in (1, 2, 3)] for axis in "xyz"}
    high = {"lat": (lat_hi, lon), "lon": (lat, lon_hi), "diag": (lat_hi, lon_hi)}
    barrier = pltpu.get_barrier_semaphore()
    greet = [(lat_lo, lon), (lat, lon_lo), (lat_lo, lon_lo), sib]
    for axis in "xyz":
        greet.extend(peers[axis])
    for dev in greet:
        pl.semaphore_signal(barrier, inc=1, device_id=dev, device_id_type=MESH)
    pl.semaphore_wait(barrier, len(greet))

    started = []

    def send(src, dst, s_sem, r_sem, dev):
        copy = pltpu.make_async_remote_copy(
            src_ref=src, dst_ref=dst, send_sem=s_sem, recv_sem=r_sem, device_id=dev, device_id_type=MESH
        )
        copy.start()
        started.append(copy)
        return copy

    flight = {}

    def send_stage(group, stage, axis, pairs):
        copies = []
        for j in range(3):
            src, dst = pairs(j)
            index = (group, stage, j)
            copies.append(send(src, dst, st_send.at[index], st_recv.at[index], peers[axis][j]))
        flight[group] = copies

    def arrived(group):
        for copy in flight[group]:
            copy.wait_recv()

    def size_of(group, level):
        return GROUPS[group][1] // (4, 16)[level]

    def start_of(group, level):
        return GROUPS[group][0] // (1, 4)[level]

    def own_rows(group, level, j=0):
        first, size = start_of(group, level), size_of(group, level)
        turn = lax.rem(co[GROUPS[group][2][level]] + j, 4)
        return pl.ds(pl.multiple_of(first + turn * size, 16), size)

    def landing(group, level):
        return pl.ds(GROUPS[group][0] // (4, 16)[level], size_of(group, level))

    def scatter(group, level, src, dst):
        def pairs(j):
            return src.at[own_rows(group, level, j + 1)], dst.at[j, landing(group, level)]

        send_stage(group, level, GROUPS[group][2][level], pairs)

    def gathered(group, level, src, dst):
        arrived(group)
        total = src[own_rows(group, level)].astype(F32)
        for j in range(3):
            total = total + dst[j, landing(group, level)].astype(F32)
        return total.astype(BF)

    def final_rows(group, level):
        first, rows, axes = GROUPS[group]
        off = first + co[axes[0]] * (rows // 4)
        if level == 1:
            off = off + co[axes[1]] * (rows // 16)
        return pl.ds(pl.multiple_of(off, 16), size_of(group, level))

    def spread(group, level):
        where = sum_ref.at[core, final_rows(group, level)]
        send_stage(group, 4 - level, GROUPS[group][2][level], lambda j: (where, where))

    sib_in = {}
    for group, (first, count, _) in enumerate(GROUPS):
        rows = pl.ds(first, count)
        sib_in[group] = send(grads_ref.at[1 - core, rows], r0.at[rows], sib_send.at[group], sib_recv.at[group], sib)

    def join(group):
        sib_in[group].wait_recv()
        rows = pl.ds(GROUPS[group][0], GROUPS[group][1])
        a1[rows] = (grads_ref[core, rows].astype(F32) + r0[rows].astype(F32)).astype(BF)

    def advance(group, stage):
        if stage == 0:
            join(group)
            scatter(group, 0, a1, r1)
        elif stage == 1:
            a2[landing(group, 0)] = gathered(group, 0, a1, r1)
            scatter(group, 1, a2, r2)
        elif stage == 2:
            me = co[GROUPS[group][2][2]]
            a3[me, landing(group, 1)] = gathered(group, 1, a2, r2)
            here = a3.at[me, landing(group, 1)]
            send_stage(group, 2, GROUPS[group][2][2], lambda j: (here, here))
        elif stage == 3:
            arrived(group)
            total = a3[0, landing(group, 1)].astype(F32)
            for i in range(1, 4):
                total = total + a3[i, landing(group, 1)].astype(F32)
            sum_ref[core, final_rows(group, 1)] = total.astype(BF)
            spread(group, 1)
        elif stage == 4:
            arrived(group)
            spread(group, 0)
        elif stage == 5:
            arrived(group)
            whole = sum_ref.at[core, pl.ds(GROUPS[group][0], GROUPS[group][1])]
            flight[group] = [send(whole, whole, sib_send.at[6 + group], sib_recv.at[6 + group], sib)]
        else:
            arrived(group)

    def small_stage(stage, values):
        axis = ("core", "x", "y", "z")[stage]
        buf = (sv0, sv1, sv2, sv3)[stage]
        me = co[axis]
        buf[me] = values
        copies = []
        for j, dev in enumerate([sib] if stage == 0 else peers[axis]):
            index = 0 if stage == 0 else 1 + 3 * (stage - 1) + j
            copies.append(send(buf.at[me], buf.at[me], sv_send.at[index], sv_recv.at[index], dev))
        return copies

    def small_sum(stage, copies):
        buf = (sv0, sv1, sv2, sv3)[stage]
        for copy in copies:
            copy.wait_recv()
        total = buf[0]
        for i in range(1, 2 if stage == 0 else 4):
            total = total + buf[i]
        return total

    small_copies = small_stage(0, small_ref[...])
    back = {}
    for i, (slot, way) in enumerate(SLOT_SENDS):
        back[slot] = send(back_ref.at[slot], ret_ref.at[slot], out_send.at[i], out_recv.at[i], high[way])
    for slot in KEPT_SLOTS:
        ret_ref[slot] = back_ref[slot]
    for stage in range(7):
        for group in range(len(GROUPS)):
            advance(group, stage)
        if stage < 3:
            small_copies = small_stage(stage + 1, small_sum(stage, small_copies))
        elif stage == 3:
            small_out_ref[...] = small_sum(3, small_copies)
    for slot in back:
        back[slot].wait_recv()
    for copy in started:
        copy.wait_send()


def finish_kernel(
    ret_ref, sum_ref, small_ref, perm_ref,
    mixed_hbm, gtok_hbm, gqkv_hbm, gproj_hbm, gain_ref, gscale_ref,
    mixed_s, gtok_s, gqkv_s, gproj_s, sems,
):
    copies = []

    def write_out(src, dst):
        copies.append(pltpu.make_async_copy(src, dst, sems.at[len(copies)]))
        copies[-1].start()

    for b in (3, 0, 1, 2):
        for half in range(2):
            rows = slice(half * 256, (half + 1) * 256)
            for ct in range(4):
                first = b * 1024 + ct * 256
                tile = sum_ref[half, first : first + 256].astype(F32)
                if b < 3:
                    gqkv_s[b, rows, ct * 128 : (ct + 1) * 128] = tile
                else:
                    gproj_s[rows, ct * 128 : (ct + 1) * 128] = tile
            where = pl.ds(half * 256, 256)
            if b < 3:
                write_out(gqkv_s.at[b, where], gqkv_hbm.at[where, pl.ds(b * 512, 512)])
            else:
                write_out(gproj_s.at[where], gproj_hbm.at[where])
    ret = ret_ref[...].astype(F32)
    perm = perm_ref[...]
    mixed = jnp.concatenate([ret[0], ret[2]] + [ret[slot][:QT] for slot in (4, 5, 6, 7)], axis=0).astype(BF)
    mixed_s[...] = dot(perm, mixed, 0, 0).astype(BF)
    write_out(mixed_s, mixed_hbm)
    gtok = jnp.concatenate([ret[1], ret[3]] + [ret[slot][QT:] for slot in (4, 5, 6, 7)], axis=0).astype(BF)
    gtok_s[...] = dot(perm, gtok, 0, 0).astype(BF)
    write_out(gtok_s, gtok_hbm)
    for i in range(4):
        gain_ref[:, i * 128 : (i + 1) * 128] = small_ref[i : i + 1, :]
    eye = lax.broadcasted_iota(jnp.int32, (8, 128), 0) == lax.broadcasted_iota(jnp.int32, (8, 128), 1)
    row = jnp.sum(jnp.where(eye, small_ref[8:16, :], 0.0), axis=0, keepdims=True)
    gscale_ref[...] = row[:, :8]
    for copy in copies:
        copy.wait()


VM = pl.BlockSpec(memory_space=pltpu.VMEM)
HBM = pl.BlockSpec(memory_space=pltpu.HBM)
DMA = pltpu.SemaphoreType.DMA
MIB = 1024 * 1024


def per_device(tokens, cotangent, key_keep, norm_gain, w_qkv, w_proj, attn_scale):
    perm, member, place = tables()
    perm = jnp.asarray(perm, BF)
    x = tokens.reshape(288, 512)
    g = cotangent.reshape(288, 512)
    operands = (
        x, g, key_keep.transpose(1, 0, 2), perm, jnp.asarray(member, BF), jnp.asarray(place, BF),
        w_qkv, w_proj, norm_gain.reshape(1, 512),
    )
    operands = [pltpu.with_memory_space_constraint(operand, pltpu.HBM) for operand in operands]
    win, wqkv_near, wproj_near, gain_near = pl.pallas_call(
        shift_in_kernel,
        out_shape=(
            jax.ShapeDtypeStruct((8, ROWS, 512), BF),
            jax.ShapeDtypeStruct((512, 1536), BF),
            jax.ShapeDtypeStruct((512, 512), BF),
            jax.ShapeDtypeStruct((1, 512), F32),
        ),
        in_specs=[HBM] * 9,
        out_specs=(VM,) * 4,
        scratch_shapes=[
            pltpu.VMEM((288, 512), BF),
            pltpu.VMEM((288, 512), BF),
            pltpu.VMEM((6, 2, 24), jnp.int32),
            pltpu.VMEM((8 * QT, 288), BF),
            pltpu.VMEM((8, 288), BF),
            pltpu.VMEM((288, 256), BF),
            pltpu.VMEM((5, ROWS, 512), BF),
            DMA((9,)),
            DMA((5,)),
            DMA((5,)),
        ],
        compiler_params=pltpu.CompilerParams(collective_id=1, has_side_effects=True, vmem_limit_bytes=12 * MIB),
        name="shift_in",
    )(*operands)

    tok = (2 * WIN, 512)
    back, grads, small = pl.pallas_call(
        compute_kernel,
        out_shape=(
            jax.ShapeDtypeStruct((8, ROWS, 512), BF),
            jax.ShapeDtypeStruct((2, 4096, 128), BF),
            jax.ShapeDtypeStruct((16, 128), F32),
        ),
        in_specs=[VM, VM, VM, VM, HBM],
        out_specs=(VM, VM, VM),
        scratch_shapes=[pltpu.SMEM((8,), F32), DMA] + [pltpu.VMEM(tok, BF)] * 4
        + [pltpu.VMEM(tok, F32)] * 2
        + [pltpu.VMEM(tok, BF)] * 2
        + [pltpu.VMEM((2, WIN, WIN), F32), pltpu.VMEM((8, 2, WIN), F32)],
        compiler_params=pltpu.CompilerParams(vmem_limit_bytes=32 * MIB),
        name="windows",
    )(win, wqkv_near, wproj_near, gain_near, pltpu.with_memory_space_constraint(attn_scale, pltpu.HBM))

    ret, total, small = pl.pallas_call(
        reduce_kernel,
        out_shape=(
            jax.ShapeDtypeStruct((8, ROWS, 512), BF),
            jax.ShapeDtypeStruct((2, 4096, 128), BF),
            jax.ShapeDtypeStruct((16, 128), F32),
        ),
        in_specs=[VM] * 3,
        out_specs=(VM,) * 3,
        scratch_shapes=[
            pltpu.VMEM((4096, 128), BF),
            pltpu.VMEM((4096, 128), BF),
            pltpu.VMEM((3, 1024, 128), BF),
            pltpu.VMEM((1024, 128), BF),
            pltpu.VMEM((3, 256, 128), BF),
            pltpu.VMEM((4, 256, 128), BF),
            pltpu.VMEM((2, 16, 128), F32),
            pltpu.VMEM((4, 16, 128), F32),
            pltpu.VMEM((4, 16, 128), F32),
            pltpu.VMEM((4, 16, 128), F32),
            DMA((5,)), DMA((5,)),
            DMA((12,)), DMA((12,)),
            DMA((6, 5, 3)), DMA((6, 5, 3)),
            DMA((10,)), DMA((10,)),
        ],
        compiler_params=pltpu.CompilerParams(collective_id=2, has_side_effects=True, vmem_limit_bytes=24 * MIB),
        name="reduce_grads",
    )(back, grads, small)

    mixed, gtok, gqkv, gproj, gain, gscale = pl.pallas_call(
        finish_kernel,
        out_shape=(
            jax.ShapeDtypeStruct((288, 512), BF),
            jax.ShapeDtypeStruct((288, 512), BF),
            jax.ShapeDtypeStruct((512, 1536), F32),
            jax.ShapeDtypeStruct((512, 512), F32),
            jax.ShapeDtypeStruct((1, 512), F32),
            jax.ShapeDtypeStruct((1, 8), F32),
        ),
        in_specs=[VM] * 4,
        out_specs=(HBM,) * 4 + (VM,) * 2,
        scratch_shapes=[
            pltpu.VMEM((288, 512), BF),
            pltpu.VMEM((288, 512), BF),
            pltpu.VMEM((3, 512, 512), F32),
            pltpu.VMEM((512, 512), F32),
            DMA((10,)),
        ],
        compiler_params=pltpu.CompilerParams(vmem_limit_bytes=24 * MIB),
        name="finish",
    )(ret, total, small, perm)
    return (
        mixed.reshape(tokens.shape),
        gtok.reshape(tokens.shape),
        gqkv,
        gproj,
        gain.reshape(512),
        gscale.reshape(8),
    )


def solution(mesh):
    grid = P(None, "lat", "lon", None)
    return jax.shard_map(
        per_device,
        mesh=mesh,
        in_specs=(grid, grid, P(None, "lat", "lon"), P(), P(), P(), P()),
        out_specs=(grid, grid, P(), P(), P(), P()),
        check_vma=False,
    )
```

time: 408 us -> 63.4 us (0.16); the launches traced: 400 us -> 63.2 us
  local copies, waits for them, and re-layouts: 104 us -> 0.01 us
  waiting for transfers between devices: 86 us -> 0 us
  blocking collectives: 65.9 us -> 0 us
  Pallas kernels: 0 us -> 62.6 us
  other arithmetic: 47.3 us -> 0 us
  starting transfers between devices: 41.4 us -> 0 us
  matrix products: 40.2 us -> 0 us
  between operations: 15.2 us -> 0.67 us
    psum x1 -> x0, waiting for transfers between devices: 82.4 us -> none  [per_device(): lax.psum((part_qkv, part_proj, d_gain, d_scale), ('lat', 'lon'))]
    psum x1 -> x0, blocking collectives: 65.9 us -> none  [per_device(): lax.psum((part_qkv, part_proj, d_gain, d_scale), ('lat', 'lon'))]
    pallas_call x0 -> x4, Pallas kernels: none -> 62.6 us  [the longest x1 33.7 us: per_device(): pl.pallas_call(reduce_kernel, out_shape=(jax.ShapeDtypeStruct((8, ROWS, 5...]
    ppermute x12 -> x0, starting transfers between devices: 41.3 us -> none  [the longest x6 22.4 us: with_halo(): lax.ppermute(lax.slice_in_dim(block, 0, width, axis=dim), axis, backward)]
    dot_general x12 -> x0, matrix products: 40.2 us -> none  [the longest x3 16.7 us: attend(): jnp.einsum('bqhd,bkhd->bhqk', query_dir, key_dir, precision=lax.Precision...]
    reshape x14 -> x0, local copies, waits for them, and re-layouts: 37.3 us -> none  [the longest x4 21 us: window_out(): kv_win = kv_win.reshape(blocks * col_wins, levels * 72, 2 * channels)]
    gather x5 -> x0, local copies, waits for them, and re-layouts: 22.5 us -> none  [the longest x4 21.9 us: window_out(): kv_ext.reshape(levels, row_wins, 6, col_wins, 12, 2 * channels)]
    slice x14 -> x0, local copies, waits for them, and re-layouts: 14.7 us -> none  [the longest x2 6.25 us: window_out(): kv_win[..., :channels]]
  transfers between devices with their start and end apart: 13 -> 0, of which waited for: 3 -> 0; matrix products, arithmetic and copies ran while one was open for 10% -> 0% of each run, Pallas kernels for 0% -> 0%
where the time goes in v1:
time: 63.4 us; the launch traced here: 63.2 us
  Pallas kernels  62.6 us (99%)
  between operations  0.67 us (1%)
    pallas_call x1, Pallas kernels, per_device(): pl.pallas_call(reduce_kernel, out_shape=(jax.ShapeDtypeStruct((8, ROWS, 5...  33.7 us
    pallas_call x1, Pallas kernels, per_device(): pl.pallas_call(shift_in_kernel, out_shape=(jax.ShapeDtypeStruct((8, ROWS,...  16.1 us
    pallas_call x1, Pallas kernels, per_device(): pl.pallas_call(compute_kernel, out_shape=(jax.ShapeDtypeStruct((8, ROWS,...  9.45 us
    pallas_call x1, Pallas kernels, per_device(): pl.pallas_call(finish_kernel, out_shape=(jax.ShapeDtypeStruct((288, 512),...  3.31 us

profile of v1, /device:TPU:1, one launch (start us, length us, event | category | flops | bytes accessed | tf_op | source)
XLA Modules:
  0.0 63.2 jit_solution(2673059095833793556)
XLA Ops:
  0.6 16.1 %shift_in.1 = (bf16[8,80,512]{2,1,0:T(8,128)(2,1)S(1)}, bf16[512,1536]{1,0:T(8,128)(2,1)S(1)}, bf16[512,512]{1,0:T(8,128)(2,1)S(1)}, f32[1,512]{1,0:T(1,128)S(1)}) custom-call(bf16[288,512]{1,0:T(8,128)(2,1)} %bitcast.8, bf16[288,512]{1,0:T(8,128)(2,1)} %bitcast.9, s32[6,2,24]{2,1,0:T(2,128)} %bitcast.10, bf16[320,288]{1,0:T(8,128)(2,1)} %constant.6.clone.perm_hbm.perm_ref, ...), custom_call_target="tpu_custom_call" | custom-call | tf_op jit(solution)/shard_map/shift_in/pallas_call | solution.py:548
  16.8 0.0 copy-start
  16.8 9.5 %windows.1 = (bf16[8,80,512]{2,1,0:T(8,128)(2,1)S(1)}, bf16[2,4096,128]{2,1,0:T(8,128)(2,1)S(1)}, f32[16,128]{1,0:T(8,128)S(1)}) custom-call(bf16[8,80,512]{2,1,0:T(8,128)(2,1)S(1)} %get-tuple-element.22.win_ref, bf16[512,1536]{1,0:T(8,128)(2,1)S(1)} %get-tuple-element.23.wqkv_ref, bf16[512,512]{1,0:T(8,128)(2,1)S(1)} %get-tuple-element.24.wproj_ref, ...), custom_call_target="tpu_custom_call" | custom-call | tf_op jit(solution)/shard_map/windows/pallas_call | solution.py:575
  26.2 33.7 %reduce_grads.1 = (bf16[8,80,512]{2,1,0:T(8,128)(2,1)S(1)}, bf16[2,4096,128]{2,1,0:T(8,128)(2,1)S(1)}, f32[16,128]{1,0:T(8,128)S(1)}) custom-call(bf16[8,80,512]{2,1,0:T(8,128)(2,1)S(1)} %get-tuple-element.26.back_ref, bf16[2,4096,128]{2,1,0:T(8,128)(2,1)S(1)} %get-tuple-element.27.grads_ref, f32[16,128]{1,0:T(8,128)S(1)} %get-tuple-element.28.small_ref), custom_call_target="tpu_custom_call" | custom-call | tf_op jit(solution)/shard_map/reduce_grads/pallas_call | solution.py:592
  59.9 0.0 copy-done
  59.9 3.3 %finish.1 = (bf16[288,512]{1,0:T(8,128)(2,1)}, bf16[288,512]{1,0:T(8,128)(2,1)}, f32[512,1536]{1,0:T(8,128)}, f32[512,512]{1,0:T(8,128)}, f32[1,512]{1,0:T(1,128)}, /*index=5*/f32[1,8]{1,0:T(1,128)}) custom-call(bf16[8,80,512]{2,1,0:T(8,128)(2,1)S(1)} %get-tuple-element.29.ret_ref, bf16[2,4096,128]{2,1,0:T(8,128)(2,1)S(1)} %get-tuple-element.30.sum_ref, ...), custom_call_target="tpu_custom_call" | custom-call | tf_op jit(solution)/shard_map/finish/pallas_call | solution.py:621
Async XLA Ops:
  16.8 43.2 %copy-start = (bf16[320,288]{1,0:T(8,128)(2,1)S(1)}, bf16[320,288]{1,0:T(8,128)(2,1)}, u32[]{:S(2)}) copy-start(bf16[320,288]{1,0:T(8,128)(2,1)} %constant.6.clone.perm_hbm.perm_ref) | copy-start | bytes 552964

commit v2 on v1

v2 whole, which is shorter than its diff:
```python
import functools

import jax
import jax.numpy as jnp
import numpy as np
from jax import lax
from jax.experimental import pallas as pl
from jax.experimental.pallas import tpu as pltpu
from jax.sharding import PartitionSpec as P

EPS_NORM = 1e-05
EPS_DIR = 1e-06
MESH = pl.DeviceIdType.MESH
BF = jnp.bfloat16
F32 = jnp.float32

QUARTERS = ((1, 1), (1, 2), (0, 1), (0, 2), (1, 3), (1, 0), (0, 3), (0, 0))
QT = 40
ROWS = 80
WIN = 160
FLAG_ROW = 36


def token_of(quarter, t):
    half, cq = QUARTERS[quarter]
    lev, rest = divmod(t, 18)
    rr, cc = divmod(rest, 6)
    return lev * 144 + (half * 3 + rr) * 24 + cq * 6 + cc


def tables():
    perm = np.zeros((8 * QT, 288), np.float32)
    member = np.zeros((8, 288), np.float32)
    place = np.zeros((288, 256), np.float32)
    for quarter in range(8):
        for t in range(36):
            src = token_of(quarter, t)
            perm[quarter * QT + t, src] = 1.0
            member[quarter, src] = 1.0
            place[src, QT * (quarter % 4) + t] = 1.0
    return perm, member, place


def dot(a, b, ca=1, cb=0):
    return lax.dot_general(a, b, (((ca,), (cb,)), ((), ())), preferred_element_type=F32)


def position():
    lat = lax.axis_index("lat")
    lon = lax.axis_index("lon")
    return lat, lon


def wrap(value, count):
    return lax.rem(value + count, count)


SLOT_SENDS = ((2, "lat"), (5, "lon"), (7, "diag"), (6, "lat"), (3, "lat"))
KEPT_SLOTS = (0, 1, 4)

GROUPS = (
    (0, 768, "xzy"),
    (768, 512, "yxz"),
    (1280, 768, "zyx"),
    (2048, 768, "xzy"),
    (2816, 512, "yxz"),
    (3328, 768, "zyx"),
)
WAVES = ((0, 1, 2), (3, 4, 5))


def slot_pieces(slot):
    if slot < 4:
        first = 2 * (slot // 2)
        kind = "xg"[slot % 2]
        return ((kind, first), (kind, first + 1))
    return (("x", slot), ("g", slot))


def coordinates():
    lat, lon = position()
    core = lax.rem(lat, 2)
    y = (lat // 2) * 2 + lon // 16
    x = lax.rem(lon // 4, 4)
    z = lax.rem(lon, 4)
    return {"x": x, "y": y, "z": z, "core": core}


def device_at(co):
    return ((co["y"] // 2) * 2 + co["core"], lax.rem(co["y"], 2) * 16 + co["x"] * 4 + co["z"])


def peer(co, axis, j):
    moved = dict(co)
    moved[axis] = lax.rem(co[axis] + j, 4)
    return device_at(moved)


def sibling(co):
    moved = dict(co)
    moved["core"] = 1 - co["core"]
    return device_at(moved)


def block_kernel(
    x_hbm, g_hbm, keep_hbm, perm_hbm, member_hbm, place_hbm, wqkv_hbm, wproj_hbm, gain_hbm, scale_hbm,
    ret_ref, sum_ref, small_out_ref,
    x_ref, g_ref, keep_ref, perm_ref, member_ref, place_ref, wqkv_ref, wproj_ref, gain_ref, scale_ref, in_buf, win_ref, back_ref,
    x_s, xh_s, rstd_s, y_s, g_s, rq_s, rk_s, rq_rows_s, q_s, k_s, qd_s, kd_s, v_s, do_s, dq_s, dk_s, dv_s, att_s, allow_s, gs_s, small_s,
    grads_ref, r0, a1, r1, a2, r2, a3, sv0, sv1, sv2, sv3,
    w_sem, in_send, in_recv, out_send, out_recv, sib_send, sib_recv, st_send, st_recv, sv_send, sv_recv,
):
    lat, lon = position()
    lat_lo, lat_hi = wrap(lat - 1, 4), wrap(lat + 1, 4)
    lon_lo, lon_hi = wrap(lon - 1, 32), wrap(lon + 1, 32)
    co = coordinates()
    core = co["core"]
    sib = sibling(co)
    peers = {axis: [peer(co, axis, j) for j in (1, 2, 3)] for axis in "xyz"}

    loads = {}
    for i, (name, src, dst) in enumerate((
        ("perm", perm_hbm, perm_ref),
        ("x", x_hbm, x_ref),
        ("keep", keep_hbm, keep_ref),
        ("member", member_hbm, member_ref),
        ("place", place_hbm, place_ref),
        ("g", g_hbm, g_ref),
        ("gain", gain_hbm, gain_ref),
        ("qkv", wqkv_hbm, wqkv_ref),
        ("proj", wproj_hbm, wproj_ref),
        ("scale", scale_hbm, scale_ref),
    )):
        loads[name] = pltpu.make_async_copy(src, dst, w_sem.at[i])
        loads[name].start()

    barrier = pltpu.get_barrier_semaphore()
    greet = [(lat_lo, lon), (lat, lon_lo), (lat_lo, lon_lo), (lat_hi, lon), (lat, lon_hi), (lat_hi, lon_hi), sib]
    for axis in "xyz":
        greet.extend(peers[axis])
    for dev in greet:
        pl.semaphore_signal(barrier, inc=1, device_id=dev, device_id_type=MESH)

    started = []

    def send(src, dst, s_sem, r_sem, dev):
        copy = pltpu.make_async_remote_copy(
            src_ref=src, dst_ref=dst, send_sem=s_sem, recv_sem=r_sem, device_id=dev, device_id_type=MESH
        )
        copy.start()
        started.append(copy)
        return copy

    for name in ("perm", "x", "keep", "member", "place", "g"):
        loads[name].wait()
    perm = perm_ref[...]
    xs = dot(perm, x_ref[...])
    gs = dot(perm, g_ref[...])
    keep_rows = [keep_ref[row, lev : lev + 1, :].astype(F32) for lev in range(2) for row in range(6)]
    marks = (jnp.concatenate(keep_rows, axis=1) * member_ref[...].astype(F32)).astype(BF)
    flags = dot(marks, place_ref[...])
    row_id = lax.broadcasted_iota(jnp.int32, (QT, 512), 0)

    def piece(kind, quarter):
        rows = slice(quarter * QT, (quarter + 1) * QT)
        if kind == "g":
            return gs[rows]
        flag = jnp.concatenate([flags[quarter : quarter + 1], jnp.zeros((1, 256), F32)], axis=1)
        return jnp.where(row_id == FLAG_ROW, flag, xs[rows])

    def payload(slot):
        return jnp.concatenate([piece(*p) for p in slot_pieces(slot)], axis=0).astype(BF)

    for i, (slot, _) in enumerate(SLOT_SENDS):
        in_buf[i] = payload(slot)
    pl.semaphore_wait(barrier, len(greet))
    low = {"lat": (lat_lo, lon), "lon": (lat, lon_lo), "diag": (lat_lo, lon_lo)}
    high = {"lat": (lat_hi, lon), "lon": (lat, lon_hi), "diag": (lat_hi, lon_hi)}
    arrive = {}
    for i, (slot, way) in enumerate(SLOT_SENDS):
        arrive[slot] = send(in_buf.at[i], win_ref.at[slot], in_send.at[i], in_recv.at[i], low[way])
    for slot in KEPT_SLOTS:
        win_ref[slot] = payload(slot)
    loads["gain"].wait()
    loads["qkv"].wait()

    gain = gain_ref[...]
    r = lax.broadcasted_iota(jnp.int32, (256, 256), 0)
    c = lax.broadcasted_iota(jnp.int32, (256, 256), 1)
    ones = jnp.where((r // 64) == (c // 64), 1.0, 0.0).astype(BF)

    r = lax.broadcasted_iota(jnp.int32, (8, 512), 0)
    c = lax.broadcasted_iota(jnp.int32, (8, 512), 1)
    head_of = jnp.where(r == c // 64, 1.0, 0.0).astype(BF)

    def head_sum(values):
        hi = values.astype(BF)
        lo = (values - hi.astype(F32)).astype(BF)
        halves = [dot(hi[:, i : i + 256], ones) + dot(lo[:, i : i + 256], ones) for i in (0, 256)]
        return jnp.concatenate(halves, axis=1)

    real = lax.broadcasted_iota(jnp.int32, (QT, 512), 0) < 36
    key_id = lax.broadcasted_iota(jnp.int32, (WIN, WIN), 0)
    query_id = lax.broadcasted_iota(jnp.int32, (WIN, WIN), 1)
    same_half = (key_id >= 2 * QT) == (query_id >= 2 * QT)
    joined = jnp.logical_or(same_half, lat != 3)
    first_row = lax.broadcasted_iota(jnp.int32, (8, WIN), 0) == 0
    one_row = jnp.where(first_row, 1.0, 0.0).astype(BF)

    def front(w):
        rows = slice(w * WIN, (w + 1) * WIN)
        if w == 0:
            data = jnp.concatenate([win_ref[0].astype(F32), win_ref[2].astype(F32)], axis=0)
        else:
            data = jnp.concatenate([win_ref[slot].astype(F32)[:QT] for slot in (4, 5, 6, 7)], axis=0)
        data = data.reshape(4, QT, 512)
        x = jnp.where(real[None], data, 0.0).reshape(WIN, 512)
        marks = data[0, FLAG_ROW : FLAG_ROW + 1, :]
        for i in range(1, 4):
            marks = marks + data[i, FLAG_ROW : FLAG_ROW + 1, :]
        marks = jnp.where(first_row, marks[:, :WIN], 0.0).astype(BF)
        keep = jnp.where(joined, dot(marks, one_row, 0, 0), 0.0)
        allow_s[w] = jnp.where(key_id == query_id, 1.0, keep)
        mean = jnp.mean(x, axis=-1, keepdims=True)
        xc = x - mean
        var = jnp.mean(xc * xc, axis=-1, keepdims=True)
        rstd = lax.rsqrt(var + EPS_NORM)
        xhat = xc * rstd
        y = (xhat * gain).astype(BF)
        x_s[rows] = x
        xh_s[rows] = xhat
        rstd_s[rows] = jnp.broadcast_to(rstd, (WIN, 128))
        y_s[rows] = y
        q_b = dot(y, wqkv_ref[:, 0:512]).astype(BF)
        k_b = dot(y, wqkv_ref[:, 512:1024]).astype(BF)
        q_s[rows] = q_b
        k_s[rows] = k_b
        q = q_b.astype(F32)
        k = k_b.astype(F32)
        v_s[rows] = dot(y, wqkv_ref[:, 1024:1536]).astype(BF)
        q_sq = q * q
        rq = lax.rsqrt(head_sum(q_sq) + EPS_DIR)
        sq_hi = q_sq.astype(BF)
        sq_lo = (q_sq - sq_hi.astype(F32)).astype(BF)
        rq_rows_s[w] = lax.rsqrt(dot(head_of, sq_hi, 1, 1) + dot(head_of, sq_lo, 1, 1) + EPS_DIR)
        rk = lax.rsqrt(head_sum(k * k) + EPS_DIR)
        rq_s[rows] = rq
        rk_s[rows] = rk
        qd_s[rows] = (q * rq).astype(BF)
        kd_s[rows] = (k * rk).astype(BF)

    arrive[2].wait_recv()
    front(0)
    for slot in (5, 7, 6):
        arrive[slot].wait_recv()
    front(1)
    arrive[3].wait_recv()
    g = jnp.concatenate(
        [win_ref[1].astype(F32), win_ref[3].astype(F32)] + [win_ref[slot].astype(F32)[QT:] for slot in (4, 5, 6, 7)],
        axis=0,
    ).astype(BF)
    g_s[...] = g
    loads["proj"].wait()
    loads["scale"].wait()
    do_s[...] = dot(g, wproj_ref[...], 1, 1).astype(BF)
    y_t = jnp.transpose(y_s[...])

    flight = {}

    def send_stage(group, stage, axis, pairs):
        copies = []
        for j in range(3):
            src, dst = pairs(j)
            index = (group, stage, j)
            copies.append(send(src, dst, st_send.at[index], st_recv.at[index], peers[axis][j]))
        flight[group] = copies

    def arrived(group):
        for copy in flight[group]:
            copy.wait_recv()

    def size_of(group, level):
        return GROUPS[group][1] // (4, 16)[level]

    def start_of(group, level):
        return GROUPS[group][0] // (1, 4)[level]

    def own_rows(group, level, j=0):
        first, size = start_of(group, level), size_of(group, level)
        turn = lax.rem(co[GROUPS[group][2][level]] + j, 4)
        return pl.ds(pl.multiple_of(first + turn * size, 16), size)

    def landing(group, level):
        return pl.ds(GROUPS[group][0] // (4, 16)[level], size_of(group, level))

    def scatter(group, level, src, dst):
        def pairs(j):
            return src.at[own_rows(group, level, j + 1)], dst.at[j, landing(group, level)]

        send_stage(group, level, GROUPS[group][2][level], pairs)

    def gathered(group, level, src, dst):
        arrived(group)
        total = src[own_rows(group, level)].astype(F32)
        for j in range(3):
            total = total + dst[j, landing(group, level)].astype(F32)
        return total.astype(BF)

    def final_rows(group, level):
        first, rows, axes = GROUPS[group]
        off = first + co[axes[0]] * (rows // 4)
        if level == 1:
            off = off + co[axes[1]] * (rows // 16)
        return pl.ds(pl.multiple_of(off, 16), size_of(group, level))

    def spread(group, level):
        where = sum_ref.at[core, final_rows(group, level)]
        send_stage(group, 4 - level, GROUPS[group][2][level], lambda j: (where, where))

    sib_in = {}

    def begin(part):
        rows = pl.ds(part * 1024, 1024)
        sib_in[part] = send(grads_ref.at[1 - core, rows], r0.at[rows], sib_send.at[part], sib_recv.at[part], sib)

    def join(part):
        sib_in[part].wait_recv()
        rows = pl.ds(part * 1024, 1024)
        a1[rows] = (grads_ref[core, rows].astype(F32) + r0[rows].astype(F32)).astype(BF)

    def advance(group, stage):
        if stage == 0:
            scatter(group, 0, a1, r1)
        elif stage == 1:
            a2[landing(group, 0)] = gathered(group, 0, a1, r1)
            scatter(group, 1, a2, r2)
        elif stage == 2:
            me = co[GROUPS[group][2][2]]
            a3[me, landing(group, 1)] = gathered(group, 1, a2, r2)
            here = a3.at[me, landing(group, 1)]
            send_stage(group, 2, GROUPS[group][2][2], lambda j: (here, here))
        elif stage == 3:
            arrived(group)
            total = a3[0, landing(group, 1)].astype(F32)
            for i in range(1, 4):
                total = total + a3[i, landing(group, 1)].astype(F32)
            sum_ref[core, final_rows(group, 1)] = total.astype(BF)
            spread(group, 1)
        elif stage == 4:
            arrived(group)
            spread(group, 0)
        elif stage == 5:
            arrived(group)
            whole = sum_ref.at[core, pl.ds(GROUPS[group][0], GROUPS[group][1])]
            flight[group] = [send(whole, whole, sib_send.at[4 + group], sib_recv.at[4 + group], sib)]
        else:
            arrived(group)

    def advance_wave(wave, stage):
        for group in WAVES[wave]:
            advance(group, stage)

    lane = lax.broadcasted_iota(jnp.int32, (1, 128), 1)
    small_ones = ones[:128, :128]

    def pair_of_heads(pair):
        cols = slice(pair * 128, (pair + 1) * 128)
        scales = [scale_ref[pair * 2 + i] for i in range(2)]
        s_lane = jnp.where(lane < 64, scales[0], scales[1])

        def window(w):
            rows = slice(w * WIN, (w + 1) * WIN)
            q_p = q_s[rows, cols]
            k_p = k_s[rows, cols]
            qd_p = qd_s[rows, cols]
            kd_p = kd_s[rows, cols]
            v_p = v_s[rows, cols]
            do_p = do_s[rows, cols]
            allow = allow_s[w]
            acc_o = jnp.zeros((WIN, 128), F32)
            acc_q = jnp.zeros((WIN, 128), F32)
            acc_k = jnp.zeros((WIN, 128), F32)
            acc_v = jnp.zeros((WIN, 128), F32)
            zero = jnp.zeros((WIN, 128), BF)
            for i in range(2):
                s = scales[i]
                mine = jnp.broadcast_to((lane < 64) if i == 0 else (lane >= 64), (WIN, 128))
                qd_h = jnp.where(mine, qd_p, zero)
                kd_h = jnp.where(mine, kd_p, zero)
                v_h = jnp.where(mine, v_p, zero)
                do_h = jnp.where(mine, do_p, zero)
                rq_row = rq_rows_s[w, pair * 2 + i : pair * 2 + i + 1, :]
                rk_col = rk_s[rows, pair * 128 + i * 64 : pair * 128 + i * 64 + 1]
                cos = dot(k_p, jnp.where(mine, q_p, zero), 1, 1) * rk_col * rq_row
                e = jnp.exp(s * cos - s) * allow
                p = e * (1.0 / jnp.sum(e, axis=0, keepdims=True))
                dp = dot(v_p, do_h, 1, 1)
                dl = p * (dp - jnp.sum(p * dp, axis=0, keepdims=True))
                gs_s[w * 4 + pair, i : i + 1, :] = jnp.sum(dl * cos, axis=0, keepdims=True)
                p_b = p.astype(BF)
                dl_b = dl.astype(BF)
                acc_o = acc_o + dot(p_b, v_h, 0, 0)
                acc_v = acc_v + dot(p_b, do_h)
                acc_k = acc_k + dot(dl_b, qd_h)
                acc_q = acc_q + dot(dl_b, kd_h, 0, 0)
            att_s[rows, cols] = acc_o.astype(BF)
            dv_s[rows, cols] = acc_v.astype(BF)
            qd = qd_p.astype(F32)
            kd = kd_p.astype(F32)
            dqd = acc_q * s_lane
            dkd = acc_k * s_lane
            dq_s[rows, cols] = (rq_s[rows, cols] * (dqd - qd * dot((qd * dqd).astype(BF), small_ones))).astype(BF)
            dk_s[rows, cols] = (rk_s[rows, cols] * (dkd - kd * dot((kd * dkd).astype(BF), small_ones))).astype(BF)

        window(0)
        window(1)
        d_all = jnp.concatenate([dq_s[:, cols], dk_s[:, cols], dv_s[:, cols]], axis=1)
        gq = dot(y_t, d_all).astype(BF)
        gp = dot(att_s[:, cols], g_s[...], 0, 0).astype(BF)
        for half in range(2):
            for i in range(3):
                first = pair * 1024 + i * 256
                grads_ref[half, first : first + 256] = gq[half * 256 : (half + 1) * 256, i * 128 : (i + 1) * 128]
            for ct in range(4):
                first = pair * 1024 + 768 + ct * 64
                grads_ref[half, first : first + 64] = gp[half * 64 : (half + 1) * 64, ct * 128 : (ct + 1) * 128]
        begin(pair)

    for pair in range(4):
        pair_of_heads(pair)
        if pair == 2:
            join(0)
            join(1)
            advance_wave(0, 0)

    def out_slot(slot, pieces):
        back_ref[slot] = jnp.concatenate(pieces, axis=0).astype(BF)

    back = {}

    def send_back(slots):
        for i, (slot, way) in enumerate(SLOT_SENDS):
            if slot in slots:
                back[slot] = send(back_ref.at[slot], ret_ref.at[slot], out_send.at[i], out_recv.at[i], high[way])

    mixed = x_s[...] + dot(att_s[...], wproj_ref[...])
    for slot in (0, 2):
        out_slot(slot, [mixed[slot * QT : (slot + 2) * QT]])
    send_back((2,))
    dn = dot(dq_s[...], wqkv_ref[:, 0:512], 1, 1)
    dn = dn + dot(dk_s[...], wqkv_ref[:, 512:1024], 1, 1)
    dn = dn + dot(dv_s[...], wqkv_ref[:, 1024:1536], 1, 1)
    xhat = xh_s[...]
    d_gain = jnp.sum(dn * xhat, axis=0, keepdims=True)
    small_s[...] = jnp.zeros((16, 128), F32)
    for i in range(4):
        small_s[i : i + 1, :] = d_gain[:, i * 128 : (i + 1) * 128]
    for h in range(8):
        row = gs_s[h // 2, h % 2 : h % 2 + 1, :] + gs_s[4 + h // 2, h % 2 : h % 2 + 1, :]
        small_s[8 + h : 9 + h, :] = jnp.broadcast_to(jnp.sum(row, axis=1, keepdims=True), (1, 128))

    def small_stage(stage, values):
        axis = ("core", "x", "y", "z")[stage]
        buf = (sv0, sv1, sv2, sv3)[stage]
        me = co[axis]
        buf[me] = values
        copies = []
        for j, dev in enumerate([sib] if stage == 0 else peers[axis]):
            index = 0 if stage == 0 else 1 + 3 * (stage - 1) + j
            copies.append(send(buf.at[me], buf.at[me], sv_send.at[index], sv_recv.at[index], dev))
        return copies

    def small_sum(stage, copies):
        buf = (sv0, sv1, sv2, sv3)[stage]
        for copy in copies:
            copy.wait_recv()
        total = buf[0]
        for i in range(1, 2 if stage == 0 else 4):
            total = total + buf[i]
        return total

    small_copies = small_stage(0, small_s[...])
    dxh = dn * gain
    rstd = rstd_s[:, 0:1]
    dx = rstd * (dxh - jnp.mean(dxh, axis=-1, keepdims=True) - xhat * jnp.mean(dxh * xhat, axis=-1, keepdims=True))
    gtok = g_s[...].astype(F32) + dx
    for slot in (1, 3):
        out_slot(slot, [gtok[(slot - 1) * QT : (slot + 1) * QT]])
    for slot in (4, 5, 6, 7):
        rows = slice(slot * QT, (slot + 1) * QT)
        out_slot(slot, [mixed[rows], gtok[rows]])
    for slot in KEPT_SLOTS:
        ret_ref[slot] = back_ref[slot]
    join(2)
    join(3)
    advance_wave(1, 0)
    send_back((5, 7, 6, 3))
    for stage in range(1, 7):
        advance_wave(0, stage)
        advance_wave(1, stage)
        if stage < 4:
            small_copies = small_stage(stage, small_sum(stage - 1, small_copies))
        elif stage == 4:
            small_out_ref[...] = small_sum(3, small_copies)
    for slot in back:
        back[slot].wait_recv()
    for copy in started:
        copy.wait_send()


def finish_kernel(ret_ref, sum_ref, small_ref, perm_ref, mixed_ref, gtok_ref, gqkv_ref, gproj_ref, gain_ref, gscale_ref):
    ret = ret_ref[...].astype(F32)
    perm = perm_ref[...]
    mixed = jnp.concatenate([ret[0], ret[2]] + [ret[slot][:QT] for slot in (4, 5, 6, 7)], axis=0).astype(BF)
    gtok = jnp.concatenate([ret[1], ret[3]] + [ret[slot][QT:] for slot in (4, 5, 6, 7)], axis=0).astype(BF)
    mixed_ref[...] = dot(perm, mixed, 0, 0).astype(BF)
    gtok_ref[...] = dot(perm, gtok, 0, 0).astype(BF)
    for half in range(2):
        for p in range(4):
            for i in range(3):
                cols = slice(i * 512 + p * 128, i * 512 + (p + 1) * 128)
                first = p * 1024 + i * 256
                tile = sum_ref[half, first : first + 256]
                gqkv_ref[half * 256 : (half + 1) * 256, cols] = tile.astype(F32)
            for ct in range(4):
                first = p * 1024 + 768 + ct * 64
                tile = sum_ref[half, first : first + 64]
                rows = slice(p * 128 + half * 64, p * 128 + (half + 1) * 64)
                gproj_ref[rows, ct * 128 : (ct + 1) * 128] = tile.astype(F32)
    for i in range(4):
        gain_ref[:, i * 128 : (i + 1) * 128] = small_ref[i : i + 1, :]
    eye = lax.broadcasted_iota(jnp.int32, (8, 128), 0) == lax.broadcasted_iota(jnp.int32, (8, 128), 1)
    row = jnp.sum(jnp.where(eye, small_ref[8:16, :], 0.0), axis=0, keepdims=True)
    gscale_ref[...] = row[:, :8]


VM = pl.BlockSpec(memory_space=pltpu.VMEM)
HBM = pl.BlockSpec(memory_space=pltpu.HBM)
DMA = pltpu.SemaphoreType.DMA
MIB = 1024 * 1024


def per_device(tokens, cotangent, key_keep, norm_gain, w_qkv, w_proj, attn_scale):
    perm, member, place = tables()
    perm = jnp.asarray(perm, BF)
    x = tokens.reshape(288, 512)
    g = cotangent.reshape(288, 512)
    tok = (2 * WIN, 512)
    operands = (
        x, g, key_keep.transpose(1, 0, 2), perm, jnp.asarray(member, BF), jnp.asarray(place, BF),
        w_qkv, w_proj, norm_gain.reshape(1, 512), attn_scale,
    )
    operands = [pltpu.with_memory_space_constraint(operand, pltpu.HBM) for operand in operands]
    ret, total, small = pl.pallas_call(
        block_kernel,
        out_shape=(
            jax.ShapeDtypeStruct((8, ROWS, 512), BF),
            jax.ShapeDtypeStruct((2, 4096, 128), BF),
            jax.ShapeDtypeStruct((16, 128), F32),
        ),
        in_specs=[HBM] * 10,
        out_specs=(VM,) * 3,
        scratch_shapes=[
            pltpu.VMEM((288, 512), BF),
            pltpu.VMEM((288, 512), BF),
            pltpu.VMEM((6, 2, 24), jnp.int32),
            pltpu.VMEM((8 * QT, 288), BF),
            pltpu.VMEM((8, 288), BF),
            pltpu.VMEM((288, 256), BF),
            pltpu.VMEM((512, 1536), BF),
            pltpu.VMEM((512, 512), BF),
            pltpu.VMEM((1, 512), F32),
            pltpu.SMEM((8,), F32),
            pltpu.VMEM((5, ROWS, 512), BF),
            pltpu.VMEM((8, ROWS, 512), BF),
            pltpu.VMEM((8, ROWS, 512), BF),
            pltpu.VMEM(tok, F32),
            pltpu.VMEM(tok, F32),
            pltpu.VMEM((2 * WIN, 128), F32),
            pltpu.VMEM(tok, BF),
            pltpu.VMEM(tok, BF),
            pltpu.VMEM(tok, F32),
            pltpu.VMEM(tok, F32),
        ]
        + [pltpu.VMEM((2, 8, WIN), F32)]
        + [pltpu.VMEM(tok, BF)] * 10
        + [
            pltpu.VMEM((2, WIN, WIN), F32),
            pltpu.VMEM((8, 2, WIN), F32),
            pltpu.VMEM((16, 128), F32),
            pltpu.VMEM((2, 4096, 128), BF),
            pltpu.VMEM((4096, 128), BF),
            pltpu.VMEM((4096, 128), BF),
            pltpu.VMEM((3, 1024, 128), BF),
            pltpu.VMEM((1024, 128), BF),
            pltpu.VMEM((3, 256, 128), BF),
            pltpu.VMEM((4, 256, 128), BF),
            pltpu.VMEM((2, 16, 128), F32),
            pltpu.VMEM((4, 16, 128), F32),
            pltpu.VMEM((4, 16, 128), F32),
            pltpu.VMEM((4, 16, 128), F32),
            DMA((10,)),
            DMA((5,)), DMA((5,)),
            DMA((5,)), DMA((5,)),
            DMA((10,)), DMA((10,)),
            DMA((6, 5, 3)), DMA((6, 5, 3)),
            DMA((10,)), DMA((10,)),
        ],
        compiler_params=pltpu.CompilerParams(collective_id=1, has_side_effects=True, vmem_limit_bytes=40 * MIB),
        name="block",
    )(*operands)

    mixed, gtok, gqkv, gproj, gain, gscale = pl.pallas_call(
        finish_kernel,
        out_shape=(
            jax.ShapeDtypeStruct((288, 512), BF),
            jax.ShapeDtypeStruct((288, 512), BF),
            jax.ShapeDtypeStruct((512, 1536), F32),
            jax.ShapeDtypeStruct((512, 512), F32),
            jax.ShapeDtypeStruct((1, 512), F32),
            jax.ShapeDtypeStruct((1, 8), F32),
        ),
        in_specs=[VM] * 4,
        out_specs=(VM,) * 6,
        compiler_params=pltpu.CompilerParams(vmem_limit_bytes=24 * MIB),
        name="finish",
    )(ret, total, small, perm)
    return (
        mixed.reshape(tokens.shape),
        gtok.reshape(tokens.shape),
        gqkv,
        gproj,
        gain.reshape(512),
        gscale.reshape(8),
    )


def solution(mesh):
    grid = P(None, "lat", "lon", None)
    return jax.shard_map(
        per_device,
        mesh=mesh,
        in_specs=(grid, grid, P(None, "lat", "lon"), P(), P(), P(), P()),
        out_specs=(grid, grid, P(), P(), P(), P()),
        check_vma=False,
    )
```

time: 63.4 us -> 55.8 us (0.88)
  Pallas kernels: 62.6 us -> 55 us
    pallas_call x3 -> x1, Pallas kernels: 59.3 us -> 52.4 us  [per_device(): pl.pallas_call(block_kernel, out_shape=(jax.ShapeDtypeStruct((8, ROWS, 51...]
    pallas_call x1, Pallas kernels: 3.31 us -> 2.62 us  [per_device(): pl.pallas_call(finish_kernel, out_shape=(jax.ShapeDtypeStruct((288, 512),...]
where the time goes in v2:
time: 55.8 us; the launch traced here: 55.7 us
  Pallas kernels  55 us (99%)
  between operations  0.66 us (1%)
    pallas_call x1, Pallas kernels, per_device(): pl.pallas_call(block_kernel, out_shape=(jax.ShapeDtypeStruct((8, ROWS, 51...  52.4 us
    pallas_call x1, Pallas kernels, per_device(): pl.pallas_call(finish_kernel, out_shape=(jax.ShapeDtypeStruct((288, 512),...  2.62 us

profile of v2, /device:TPU:1, one launch (start us, length us, event | category | flops | bytes accessed | tf_op | source)
XLA Modules:
  0.0 55.7 jit_solution(11160476696827445211)
XLA Ops:
  0.6 0.0 copy-start
  0.6 52.4 %block.1 = (bf16[8,80,512]{2,1,0:T(8,128)(2,1)S(1)}, bf16[2,4096,128]{2,1,0:T(8,128)(2,1)S(1)}, f32[16,128]{1,0:T(8,128)S(1)}) custom-call(bf16[288,512]{1,0:T(8,128)(2,1)} %bitcast.8, bf16[288,512]{1,0:T(8,128)(2,1)} %bitcast.9, s32[6,2,24]{2,1,0:T(2,128)} %bitcast.10, bf16[320,288]{1,0:T(8,128)(2,1)} %constant.6.clone.perm_hbm.perm_ref, ...), custom_call_target="tpu_custom_call" | custom-call | tf_op jit(solution)/shard_map/block/pallas_call | solution.py:554
  53.0 0.0 copy-done
  53.0 2.6 %finish.1 = (bf16[288,512]{1,0:T(8,128)(2,1)}, bf16[288,512]{1,0:T(8,128)(2,1)}, f32[512,1536]{1,0:T(8,128)}, f32[512,512]{1,0:T(8,128)}, f32[1,512]{1,0:T(1,128)}, /*index=5*/f32[1,8]{1,0:T(1,128)}) custom-call(bf16[8,80,512]{2,1,0:T(8,128)(2,1)S(1)} %get-tuple-element.15.ret_ref, bf16[2,4096,128]{2,1,0:T(8,128)(2,1)S(1)} %get-tuple-element.16.sum_ref, ...), custom_call_target="tpu_custom_call" | custom-call | tf_op jit(solution)/shard_map/finish/pallas_call | solution.py:613
Async XLA Ops:
  0.6 52.4 %copy-start = (bf16[320,288]{1,0:T(8,128)(2,1)S(1)}, bf16[320,288]{1,0:T(8,128)(2,1)}, u32[]{:S(2)}) copy-start(bf16[320,288]{1,0:T(8,128)(2,1)} %constant.6.clone.perm_hbm.perm_ref) | copy-start | bytes 552964

commit v3 on v2

--- a/solution.py
+++ b/solution.py
@@ -59,14 +59,18 @@
 KEPT_SLOTS = (0, 1, 4)
 
 GROUPS = (
-    (0, 768, "xzy"),
-    (768, 512, "yxz"),
-    (1280, 768, "zyx"),
-    (2048, 768, "xzy"),
-    (2816, 512, "yxz"),
-    (3328, 768, "zyx"),
+    (0, 704, "xzy"),
+    (704, 640, "yxz"),
+    (1344, 704, "zyx"),
+    (2048, 384, "xzy"),
+    (2432, 256, "yxz"),
+    (2688, 384, "zyx"),
+    (3072, 384, "xzy"),
+    (3456, 256, "yxz"),
+    (3712, 384, "zyx"),
 )
-WAVES = ((0, 1, 2), (3, 4, 5))
+WAVES = ((0, 1, 2), (3, 4, 5), (6, 7, 8))
+WAVE_PAIRS = ((0, 1), (2,), (3,))
 
 
 def slot_pieces(slot):
@@ -104,10 +108,11 @@
 
 def block_kernel(
     x_hbm, g_hbm, keep_hbm, perm_hbm, member_hbm, place_hbm, wqkv_hbm, wproj_hbm, gain_hbm, scale_hbm,
-    ret_ref, sum_ref, small_out_ref,
+    mixed_ref, gtok_ref, gqkv_ref, gproj_ref, gain_out_ref, gscale_ref,
+    ret_ref, sum_ref,
     x_ref, g_ref, keep_ref, perm_ref, member_ref, place_ref, wqkv_ref, wproj_ref, gain_ref, scale_ref, in_buf, win_ref, back_ref,
     x_s, xh_s, rstd_s, y_s, g_s, rq_s, rk_s, rq_rows_s, q_s, k_s, qd_s, kd_s, v_s, do_s, dq_s, dk_s, dv_s, att_s, allow_s, gs_s, small_s,
-    grads_ref, r0, a1, r1, a2, r2, a3, sv0, sv1, sv2, sv3,
+    grads_ref, r0, a1, r1, a2, a3, sv0, sv1, sv2, sv3,
     w_sem, in_send, in_recv, out_send, out_recv, sib_send, sib_recv, st_send, st_recv, sv_send, sv_recv,
 ):
     lat, lon = position()
@@ -279,43 +284,28 @@
         for copy in flight[group]:
             copy.wait_recv()
 
-    def size_of(group, level):
-        return GROUPS[group][1] // (4, 16)[level]
-
-    def start_of(group, level):
-        return GROUPS[group][0] // (1, 4)[level]
-
-    def own_rows(group, level, j=0):
-        first, size = start_of(group, level), size_of(group, level)
-        turn = lax.rem(co[GROUPS[group][2][level]] + j, 4)
+    def own_rows(group, j=0):
+        first, rows, axes = GROUPS[group]
+        size = rows // 4
+        turn = lax.rem(co[axes[0]] + j, 4)
         return pl.ds(pl.multiple_of(first + turn * size, 16), size)
 
-    def landing(group, level):
-        return pl.ds(GROUPS[group][0] // (4, 16)[level], size_of(group, level))
-
-    def scatter(group, level, src, dst):
-        def pairs(j):
-            return src.at[own_rows(group, level, j + 1)], dst.at[j, landing(group, level)]
-
-        send_stage(group, level, GROUPS[group][2][level], pairs)
-
-    def gathered(group, level, src, dst):
+    def landing(group):
+        return pl.ds(GROUPS[group][0] // 4, GROUPS[group][1] // 4)
+
+    def exchange(group, stage, buf, total):
+        axis = GROUPS[group][2][stage]
+        me = co[axis]
+        buf[me, landing(group)] = total.astype(BF)
+        here = buf.at[me, landing(group)]
+        send_stage(group, stage, axis, lambda j: (here, here))
+
+    def exchanged(group, buf):
         arrived(group)
-        total = src[own_rows(group, level)].astype(F32)
-        for j in range(3):
-            total = total + dst[j, landing(group, level)].astype(F32)
-        return total.astype(BF)
-
-    def final_rows(group, level):
-        first, rows, axes = GROUPS[group]
-        off = first + co[axes[0]] * (rows // 4)
-        if level == 1:
-            off = off + co[axes[1]] * (rows // 16)
-        return pl.ds(pl.multiple_of(off, 16), size_of(group, level))
-
-    def spread(group, level):
-        where = sum_ref.at[core, final_rows(group, level)]
-        send_stage(group, 4 - level, GROUPS[group][2][level], lambda j: (where, where))
+        total = buf[0, landing(group)].astype(F32)
+        for i in range(1, 4):
+            total = total + buf[i, landing(group)].astype(F32)
+        return total
 
     sib_in = {}
 
@@ -330,31 +320,38 @@
 
     def advance(group, stage):
         if stage == 0:
-            scatter(group, 0, a1, r1)
+            send_stage(
+                group, 0, GROUPS[group][2][0], lambda j: (a1.at[own_rows(group, j + 1)], r1.at[j, landing(group)])
+            )
         elif stage == 1:
-            a2[landing(group, 0)] = gathered(group, 0, a1, r1)
-            scatter(group, 1, a2, r2)
+            arrived(group)
+            total = a1[own_rows(group)].astype(F32)
+            for j in range(3):
+                total = total + r1[j, landing(group)].astype(F32)
+            exchange(group, 1, a2, total)
         elif stage == 2:
-            me = co[GROUPS[group][2][2]]
-            a3[me, landing(group, 1)] = gathered(group, 1, a2, r2)
-            here = a3.at[me, landing(group, 1)]
-            send_stage(group, 2, GROUPS[group][2][2], lambda j: (here, here))
+            exchange(group, 2, a3, exchanged(group, a2))
         elif stage == 3:
-            arrived(group)
-            total = a3[0, landing(group, 1)].astype(F32)
-            for i in range(1, 4):
-                total = total + a3[i, landing(group, 1)].astype(F32)
-            sum_ref[core, final_rows(group, 1)] = total.astype(BF)
-            spread(group, 1)
+            sum_ref[core, own_rows(group)] = exchanged(group, a3).astype(BF)
+            where = sum_ref.at[core, own_rows(group)]
+            send_stage(group, 3, GROUPS[group][2][0], lambda j: (where, where))
         elif stage == 4:
-            arrived(group)
-            spread(group, 0)
-        elif stage == 5:
             arrived(group)
             whole = sum_ref.at[core, pl.ds(GROUPS[group][0], GROUPS[group][1])]
             flight[group] = [send(whole, whole, sib_send.at[4 + group], sib_recv.at[4 + group], sib)]
         else:
             arrived(group)
+
+    def widen(pair):
+        for half in range(2):
+            for i in range(3):
+                first = pair * 1024 + i * 256
+                cols = slice(i * 512 + pair * 128, i * 512 + (pair + 1) * 128)
+                gqkv_ref[half * 256 : (half + 1) * 256, cols] = sum_ref[half, first : first + 256].astype(F32)
+            rows = slice(pair * 128 + half * 64, pair * 128 + (half + 1) * 64)
+            for ct in range(4):
+                first = pair * 1024 + 768 + ct * 64
+                gproj_ref[rows, ct * 128 : (ct + 1) * 128] = sum_ref[half, first : first + 64].astype(F32)
 
     def advance_wave(wave, stage):
         for group in WAVES[wave]:
@@ -432,6 +429,9 @@
             join(0)
             join(1)
             advance_wave(0, 0)
+        elif pair == 3:
+            join(2)
+            advance_wave(1, 0)
 
     def out_slot(slot, pieces):
         back_ref[slot] = jnp.concatenate(pieces, axis=0).astype(BF)
@@ -491,47 +491,43 @@
         out_slot(slot, [mixed[rows], gtok[rows]])
     for slot in KEPT_SLOTS:
         ret_ref[slot] = back_ref[slot]
-    join(2)
     join(3)
-    advance_wave(1, 0)
+    advance_wave(2, 0)
     send_back((5, 7, 6, 3))
-    for stage in range(1, 7):
-        advance_wave(0, stage)
-        advance_wave(1, stage)
+    for stage in range(1, 6):
+        for wave in range(3):
+            advance_wave(wave, stage)
+            if stage == 5:
+                for pair in WAVE_PAIRS[wave]:
+                    widen(pair)
         if stage < 4:
             small_copies = small_stage(stage, small_sum(stage - 1, small_copies))
-        elif stage == 4:
-            small_out_ref[...] = small_sum(3, small_copies)
-    for slot in back:
-        back[slot].wait_recv()
+        if stage == 4:
+            small = small_sum(3, small_copies)
+            for i in range(4):
+                gain_out_ref[:, i * 128 : (i + 1) * 128] = small[i : i + 1, :]
+            eye = lax.broadcasted_iota(jnp.int32, (8, 128), 0) == lax.broadcasted_iota(jnp.int32, (8, 128), 1)
+            gscale_ref[...] = jnp.sum(jnp.where(eye, small[8:16, :], 0.0), axis=0, keepdims=True)
+        if stage == 2:
+            for slot in back:
+                back[slot].wait_recv()
+            ret = [ret_ref[slot].astype(F32) for slot in range(8)]
+            out = jnp.concatenate([ret[0], ret[2]] + [ret[slot][:QT] for slot in (4, 5, 6, 7)], axis=0).astype(BF)
+            mixed_ref[...] = dot(perm_ref[...], out, 0, 0).astype(BF)
+            out = jnp.concatenate([ret[1], ret[3]] + [ret[slot][QT:] for slot in (4, 5, 6, 7)], axis=0).astype(BF)
+            gtok_ref[...] = dot(perm_ref[...], out, 0, 0).astype(BF)
     for copy in started:
         copy.wait_send()
 
 
-def finish_kernel(ret_ref, sum_ref, small_ref, perm_ref, mixed_ref, gtok_ref, gqkv_ref, gproj_ref, gain_ref, gscale_ref):
-    ret = ret_ref[...].astype(F32)
-    perm = perm_ref[...]
-    mixed = jnp.concatenate([ret[0], ret[2]] + [ret[slot][:QT] for slot in (4, 5, 6, 7)], axis=0).astype(BF)
-    gtok = jnp.concatenate([ret[1], ret[3]] + [ret[slot][QT:] for slot in (4, 5, 6, 7)], axis=0).astype(BF)
-    mixed_ref[...] = dot(perm, mixed, 0, 0).astype(BF)
-    gtok_ref[...] = dot(perm, gtok, 0, 0).astype(BF)
-    for half in range(2):
-        for p in range(4):
-            for i in range(3):
-                cols = slice(i * 512 + p * 128, i * 512 + (p + 1) * 128)
-                first = p * 1024 + i * 256
-                tile = sum_ref[half, first : first + 256]
-                gqkv_ref[half * 256 : (half + 1) * 256, cols] = tile.astype(F32)
-            for ct in range(4):
-                first = p * 1024 + 768 + ct * 64
-                tile = sum_ref[half, first : first + 64]
-                rows = slice(p * 128 + half * 64, p * 128 + (half + 1) * 64)
-                gproj_ref[rows, ct * 128 : (ct + 1) * 128] = tile.astype(F32)
-    for i in range(4):
-        gain_ref[:, i * 128 : (i + 1) * 128] = small_ref[i : i + 1, :]
-    eye = lax.broadcasted_iota(jnp.int32, (8, 128), 0) == lax.broadcasted_iota(jnp.int32, (8, 128), 1)
-    row = jnp.sum(jnp.where(eye, small_ref[8:16, :], 0.0), axis=0, keepdims=True)
-    gscale_ref[...] = row[:, :8]
+def finish_kernel(*refs):
+    sources, targets, sems = refs[:6], refs[6:12], refs[12]
+    copies = [pltpu.make_async_copy(sources[i], targets[i], sems.at[i]) for i in range(5)]
+    for copy in copies:
+        copy.start()
+    targets[5][...] = sources[5][:, :8]
+    for copy in copies:
+        copy.wait()
 
 
 VM = pl.BlockSpec(memory_space=pltpu.VMEM)
@@ -551,16 +547,22 @@
         w_qkv, w_proj, norm_gain.reshape(1, 512), attn_scale,
     )
     operands = [pltpu.with_memory_space_constraint(operand, pltpu.HBM) for operand in operands]
-    ret, total, small = pl.pallas_call(
+    results = (
+        jax.ShapeDtypeStruct((288, 512), BF),
+        jax.ShapeDtypeStruct((288, 512), BF),
+        jax.ShapeDtypeStruct((512, 1536), F32),
+        jax.ShapeDtypeStruct((512, 512), F32),
+        jax.ShapeDtypeStruct((1, 512), F32),
+        jax.ShapeDtypeStruct((1, 128), F32),
+    )
+    near = pl.pallas_call(
         block_kernel,
-        out_shape=(
-            jax.ShapeDtypeStruct((8, ROWS, 512), BF),
-            jax.ShapeDtypeStruct((2, 4096, 128), BF),
-            jax.ShapeDtypeStruct((16, 128), F32),
-        ),
+        out_shape=results,
         in_specs=[HBM] * 10,
-        out_specs=(VM,) * 3,
+        out_specs=(VM,) * 6,
         scratch_shapes=[
+            pltpu.VMEM((8, ROWS, 512), BF),
+            pltpu.VMEM((2, 4096, 128), BF),
             pltpu.VMEM((288, 512), BF),
             pltpu.VMEM((288, 512), BF),
             pltpu.VMEM((6, 2, 24), jnp.int32),
@@ -592,9 +594,8 @@
             pltpu.VMEM((4096, 128), BF),
             pltpu.VMEM((4096, 128), BF),
             pltpu.VMEM((3, 1024, 128), BF),
-            pltpu.VMEM((1024, 128), BF),
-            pltpu.VMEM((3, 256, 128), BF),
-            pltpu.VMEM((4, 256, 128), BF),
+            pltpu.VMEM((4, 1024, 128), BF),
+            pltpu.VMEM((4, 1024, 128), BF),
             pltpu.VMEM((2, 16, 128), F32),
             pltpu.VMEM((4, 16, 128), F32),
             pltpu.VMEM((4, 16, 128), F32),
@@ -602,8 +603,8 @@
             DMA((10,)),
             DMA((5,)), DMA((5,)),
             DMA((5,)), DMA((5,)),
-            DMA((10,)), DMA((10,)),
-            DMA((6, 5, 3)), DMA((6, 5, 3)),
+            DMA((13,)), DMA((13,)),
+            DMA((9, 4, 3)), DMA((9, 4, 3)),
             DMA((10,)), DMA((10,)),
         ],
         compiler_params=pltpu.CompilerParams(collective_id=1, has_side_effects=True, vmem_limit_bytes=40 * MIB),
@@ -612,19 +613,13 @@
 
     mixed, gtok, gqkv, gproj, gain, gscale = pl.pallas_call(
         finish_kernel,
-        out_shape=(
-            jax.ShapeDtypeStruct((288, 512), BF),
-            jax.ShapeDtypeStruct((288, 512), BF),
-            jax.ShapeDtypeStruct((512, 1536), F32),
-            jax.ShapeDtypeStruct((512, 512), F32),
-            jax.ShapeDtypeStruct((1, 512), F32),
-            jax.ShapeDtypeStruct((1, 8), F32),
-        ),
-        in_specs=[VM] * 4,
-        out_specs=(VM,) * 6,
-        compiler_params=pltpu.CompilerParams(vmem_limit_bytes=24 * MIB),
+        out_shape=results[:5] + (jax.ShapeDtypeStruct((1, 8), F32),),
+        in_specs=[VM] * 6,
+        out_specs=(HBM,) * 5 + (VM,),
+        scratch_shapes=[DMA((5,))],
+        compiler_params=pltpu.CompilerParams(vmem_limit_bytes=8 * MIB),
         name="finish",
-    )(ret, total, small, perm)
+    )(*near)
     return (
         mixed.reshape(tokens.shape),
         gtok.reshape(tokens.shape),

time: 55.8 us -> 57.4 us (1.029)
  Pallas kernels: 55 us -> 56.6 us
    pallas_call x2, Pallas kernels: 55 us -> 56.6 us  [the longest x1 53.8 us: per_device(): pl.pallas_call(block_kernel, out_shape=results, in_specs=[HBM] * 10, out_...]
where the time goes in v3:
time: 57.4 us; the launch traced here: 57.2 us
  Pallas kernels  56.6 us (99%)
  between operations  0.64 us (1%)
    pallas_call x1, Pallas kernels, per_device(): pl.pallas_call(block_kernel, out_shape=results, in_specs=[HBM] * 10, out_...  53.8 us
    pallas_call x1, Pallas kernels, per_device(): pl.pallas_call(finish_kernel, out_shape=results[:5] + (jax.ShapeDtypeStru...  2.76 us

profile of v3, /device:TPU:1, one launch (start us, length us, event | category | flops | bytes accessed | tf_op | source)
XLA Modules:
  0.0 57.2 jit_solution(13281907324263166027)
XLA Ops:
  0.6 53.8 %block.1 = (bf16[288,512]{1,0:T(8,128)(2,1)S(1)}, bf16[288,512]{1,0:T(8,128)(2,1)S(1)}, f32[512,1536]{1,0:T(8,128)S(1)}, f32[512,512]{1,0:T(8,128)S(1)}, f32[1,512]{1,0:T(1,128)S(1)}, /*index=5*/f32[1,128]{1,0:T(1,128)S(1)}) custom-call(bf16[288,512]{1,0:T(8,128)(2,1)} %bitcast.8, bf16[288,512]{1,0:T(8,128)(2,1)} %bitcast.9, s32[6,2,24]{2,1,0:T(2,128)} %bitcast.10, ...), custom_call_target="tpu_custom_call" | custom-call | tf_op jit(solution)/shard_map/block/pallas_call | solution.py:558
  54.5 2.8 %finish.1 = (bf16[288,512]{1,0:T(8,128)(2,1)}, bf16[288,512]{1,0:T(8,128)(2,1)}, f32[512,1536]{1,0:T(8,128)}, f32[512,512]{1,0:T(8,128)}, f32[1,512]{1,0:T(1,128)}, /*index=5*/f32[1,8]{1,0:T(1,128)}) custom-call(bf16[288,512]{1,0:T(8,128)(2,1)S(1)} %get-tuple-element.18.refs_0_, bf16[288,512]{1,0:T(8,128)(2,1)S(1)} %get-tuple-element.19.refs_1_, ...), custom_call_target="tpu_custom_call" | custom-call | tf_op jit(solution)/shard_map/finish/pallas_call | solution.py:614

commit v4 on v2

--- a/solution.py
+++ b/solution.py
@@ -58,13 +58,15 @@
 SLOT_SENDS = ((2, "lat"), (5, "lon"), (7, "diag"), (6, "lat"), (3, "lat"))
 KEPT_SLOTS = (0, 1, 4)
 
+BLOCKS = {"A": (("x", "even"), ("y", "even")), "B": (("x", "odd"), ("z", "odd")), "C": (("y", "odd"), ("z", "even"))}
+
 GROUPS = (
-    (0, 768, "xzy"),
-    (768, 512, "yxz"),
-    (1280, 768, "zyx"),
-    (2048, 768, "xzy"),
-    (2816, 512, "yxz"),
-    (3328, 768, "zyx"),
+    (0, 768, "ABC"),
+    (768, 512, "CAB"),
+    (1280, 768, "BCA"),
+    (2048, 768, "ABC"),
+    (2816, 512, "CAB"),
+    (3328, 768, "BCA"),
 )
 WAVES = ((0, 1, 2), (3, 4, 5))
 
@@ -90,10 +92,26 @@
     return ((co["y"] // 2) * 2 + co["core"], lax.rem(co["y"], 2) * 16 + co["x"] * 4 + co["z"])
 
 
-def peer(co, axis, j):
-    moved = dict(co)
-    moved[axis] = lax.rem(co[axis] + j, 4)
-    return device_at(moved)
+def pair_bit(at, kind):
+    return lax.rem(at // 2 + at, 2) if kind == "even" else at // 2
+
+
+def pair_mate(at, kind):
+    return at + 1 - 2 * lax.rem(at, 2) if kind == "even" else 3 - at
+
+
+def block_members(co, name):
+    members = []
+    for flip in range(4):
+        moved, index = dict(co), 0
+        for i, (axis, kind) in enumerate(BLOCKS[name]):
+            bit = pair_bit(co[axis], kind)
+            if flip >> i & 1:
+                moved[axis] = pair_mate(co[axis], kind)
+                bit = 1 - bit
+            index = index + bit * (1 << i)
+        members.append((index, device_at(moved)))
+    return members
 
 
 def sibling(co):
@@ -116,7 +134,11 @@
     co = coordinates()
     core = co["core"]
     sib = sibling(co)
-    peers = {axis: [peer(co, axis, j) for j in (1, 2, 3)] for axis in "xyz"}
+    peers, turns = {}, {}
+    for name in BLOCKS:
+        members = block_members(co, name)
+        turns[name] = [index for index, _ in members]
+        peers[name] = [dev for _, dev in members[1:]]
 
     loads = {}
     for i, (name, src, dst) in enumerate((
@@ -136,8 +158,8 @@
 
     barrier = pltpu.get_barrier_semaphore()
     greet = [(lat_lo, lon), (lat, lon_lo), (lat_lo, lon_lo), (lat_hi, lon), (lat, lon_hi), (lat_hi, lon_hi), sib]
-    for axis in "xyz":
-        greet.extend(peers[axis])
+    for name in BLOCKS:
+        greet.extend(peers[name])
     for dev in greet:
         pl.semaphore_signal(barrier, inc=1, device_id=dev, device_id_type=MESH)
 
@@ -287,7 +309,7 @@
 
     def own_rows(group, level, j=0):
         first, size = start_of(group, level), size_of(group, level)
-        turn = lax.rem(co[GROUPS[group][2][level]] + j, 4)
+        turn = turns[GROUPS[group][2][level]][j]
         return pl.ds(pl.multiple_of(first + turn * size, 16), size)
 
     def landing(group, level):
@@ -308,9 +330,9 @@
 
     def final_rows(group, level):
         first, rows, axes = GROUPS[group]
-        off = first + co[axes[0]] * (rows // 4)
+        off = first + turns[axes[0]][0] * (rows // 4)
         if level == 1:
-            off = off + co[axes[1]] * (rows // 16)
+            off = off + turns[axes[1]][0] * (rows // 16)
         return pl.ds(pl.multiple_of(off, 16), size_of(group, level))
 
     def spread(group, level):
@@ -335,7 +357,7 @@
             a2[landing(group, 0)] = gathered(group, 0, a1, r1)
             scatter(group, 1, a2, r2)
         elif stage == 2:
-            me = co[GROUPS[group][2][2]]
+            me = turns[GROUPS[group][2][2]][0]
             a3[me, landing(group, 1)] = gathered(group, 1, a2, r2)
             here = a3.at[me, landing(group, 1)]
             send_stage(group, 2, GROUPS[group][2][2], lambda j: (here, here))
@@ -460,9 +482,9 @@
         small_s[8 + h : 9 + h, :] = jnp.broadcast_to(jnp.sum(row, axis=1, keepdims=True), (1, 128))
 
     def small_stage(stage, values):
-        axis = ("core", "x", "y", "z")[stage]
+        axis = ("core", "A", "B", "C")[stage]
         buf = (sv0, sv1, sv2, sv3)[stage]
-        me = co[axis]
+        me = core if stage == 0 else turns[axis][0]
         buf[me] = values
         copies = []
         for j, dev in enumerate([sib] if stage == 0 else peers[axis]):

time: 55.8 us -> 58.9 us (1.056)
  Pallas kernels: 55 us -> 58.1 us
    pallas_call x1, Pallas kernels: 52.4 us -> 55.5 us  [per_device(): pl.pallas_call(block_kernel, out_shape=(jax.ShapeDtypeStruct((8, ROWS, 51...]
where the time goes in v4:
time: 58.9 us; the launch traced here: 58.8 us
  Pallas kernels  58.1 us (99%)
  between operations  0.66 us (1%)
    pallas_call x1, Pallas kernels, per_device(): pl.pallas_call(block_kernel, out_shape=(jax.ShapeDtypeStruct((8, ROWS, 51...  55.5 us
    pallas_call x1, Pallas kernels, per_device(): pl.pallas_call(finish_kernel, out_shape=(jax.ShapeDtypeStruct((288, 512),...  2.62 us

profile of v4, /device:TPU:1, one launch (start us, length us, event | category | flops | bytes accessed | tf_op | source)
XLA Modules:
  0.0 58.8 jit_solution(66639962161131123)
XLA Ops:
  0.6 0.0 copy-start
  0.6 55.5 %block.1 = (bf16[8,80,512]{2,1,0:T(8,128)(2,1)S(1)}, bf16[2,4096,128]{2,1,0:T(8,128)(2,1)S(1)}, f32[16,128]{1,0:T(8,128)S(1)}) custom-call(bf16[288,512]{1,0:T(8,128)(2,1)} %bitcast.8, bf16[288,512]{1,0:T(8,128)(2,1)} %bitcast.9, s32[6,2,24]{2,1,0:T(2,128)} %bitcast.10, bf16[320,288]{1,0:T(8,128)(2,1)} %constant.6.clone.perm_hbm.perm_ref, ...), custom_call_target="tpu_custom_call" | custom-call | tf_op jit(solution)/shard_map/block/pallas_call | solution.py:576
  56.2 0.0 copy-done
  56.2 2.6 %finish.1 = (bf16[288,512]{1,0:T(8,128)(2,1)}, bf16[288,512]{1,0:T(8,128)(2,1)}, f32[512,1536]{1,0:T(8,128)}, f32[512,512]{1,0:T(8,128)}, f32[1,512]{1,0:T(1,128)}, /*index=5*/f32[1,8]{1,0:T(1,128)}) custom-call(bf16[8,80,512]{2,1,0:T(8,128)(2,1)S(1)} %get-tuple-element.15.ret_ref, bf16[2,4096,128]{2,1,0:T(8,128)(2,1)S(1)} %get-tuple-element.16.sum_ref, ...), custom_call_target="tpu_custom_call" | custom-call | tf_op jit(solution)/shard_map/finish/pallas_call | solution.py:635
Async XLA Ops:
  0.6 55.6 %copy-start = (bf16[320,288]{1,0:T(8,128)(2,1)S(1)}, bf16[320,288]{1,0:T(8,128)(2,1)}, u32[]{:S(2)}) copy-start(bf16[320,288]{1,0:T(8,128)(2,1)} %constant.6.clone.perm_hbm.perm_ref) | copy-start | bytes 552964

commit v5 on v2

--- a/solution.py
+++ b/solution.py
@@ -62,11 +62,14 @@
     (0, 768, "xzy"),
     (768, 512, "yxz"),
     (1280, 768, "zyx"),
-    (2048, 768, "xzy"),
-    (2816, 512, "yxz"),
-    (3328, 768, "zyx"),
+    (2048, 512, "xzy"),
+    (2560, 256, "yxz"),
+    (2816, 256, "zyx"),
+    (3072, 256, "xzy"),
+    (3328, 256, "yxz"),
+    (3584, 512, "zyx"),
 )
-WAVES = ((0, 1, 2), (3, 4, 5))
+WAVES = ((0, 1, 2), (3, 4, 5), (6, 7, 8))
 
 
 def slot_pieces(slot):
@@ -132,6 +135,8 @@
         ("scale", scale_hbm, scale_ref),
     )):
         loads[name] = pltpu.make_async_copy(src, dst, w_sem.at[i])
+    first_loads = ("x", "perm", "keep", "member", "place", "g")
+    for name in first_loads:
         loads[name].start()
 
     barrier = pltpu.get_barrier_semaphore()
@@ -151,8 +156,10 @@
         started.append(copy)
         return copy
 
-    for name in ("perm", "x", "keep", "member", "place", "g"):
+    for name in first_loads:
         loads[name].wait()
+    for name in ("gain", "qkv", "proj", "scale"):
+        loads[name].start()
     perm = perm_ref[...]
     xs = dot(perm, x_ref[...])
     gs = dot(perm, g_ref[...])
@@ -432,6 +439,9 @@
             join(0)
             join(1)
             advance_wave(0, 0)
+        elif pair == 3:
+            join(2)
+            advance_wave(1, 0)
 
     def out_slot(slot, pieces):
         back_ref[slot] = jnp.concatenate(pieces, axis=0).astype(BF)
@@ -491,13 +501,17 @@
         out_slot(slot, [mixed[rows], gtok[rows]])
     for slot in KEPT_SLOTS:
         ret_ref[slot] = back_ref[slot]
-    join(2)
+    advance_wave(0, 1)
     join(3)
-    advance_wave(1, 0)
+    advance_wave(2, 0)
+    advance_wave(1, 1)
     send_back((5, 7, 6, 3))
     for stage in range(1, 7):
-        advance_wave(0, stage)
-        advance_wave(1, stage)
+        if stage < 6:
+            advance_wave(0, stage + 1)
+        advance_wave(2, stage)
+        if stage < 6:
+            advance_wave(1, stage + 1)
         if stage < 4:
             small_copies = small_stage(stage, small_sum(stage - 1, small_copies))
         elif stage == 4:
@@ -602,8 +616,8 @@
             DMA((10,)),
             DMA((5,)), DMA((5,)),
             DMA((5,)), DMA((5,)),
-            DMA((10,)), DMA((10,)),
-            DMA((6, 5, 3)), DMA((6, 5, 3)),
+            DMA((13,)), DMA((13,)),
+            DMA((9, 5, 3)), DMA((9, 5, 3)),
             DMA((10,)), DMA((10,)),
         ],
         compiler_params=pltpu.CompilerParams(collective_id=1, has_side_effects=True, vmem_limit_bytes=40 * MIB),

time: 55.8 us -> 58.3 us (1.045)
  Pallas kernels: 55 us -> 57.5 us
    pallas_call x1, Pallas kernels: 52.4 us -> 54.8 us  [per_device(): pl.pallas_call(block_kernel, out_shape=(jax.ShapeDtypeStruct((8, ROWS, 51...]
where the time goes in v5:
time: 58.3 us; the launch traced here: 58.1 us
  Pallas kernels  57.5 us (99%)
  between operations  0.66 us (1%)
    pallas_call x1, Pallas kernels, per_device(): pl.pallas_call(block_kernel, out_shape=(jax.ShapeDtypeStruct((8, ROWS, 51...  54.8 us
    pallas_call x1, Pallas kernels, per_device(): pl.pallas_call(finish_kernel, out_shape=(jax.ShapeDtypeStruct((288, 512),...  2.62 us

profile of v5, /device:TPU:1, one launch (start us, length us, event | category | flops | bytes accessed | tf_op | source)
XLA Modules:
  0.0 58.1 jit_solution(14226303145155797358)
XLA Ops:
  0.6 0.0 copy-start
  0.6 54.8 %block.1 = (bf16[8,80,512]{2,1,0:T(8,128)(2,1)S(1)}, bf16[2,4096,128]{2,1,0:T(8,128)(2,1)S(1)}, f32[16,128]{1,0:T(8,128)S(1)}) custom-call(bf16[288,512]{1,0:T(8,128)(2,1)} %bitcast.8, bf16[288,512]{1,0:T(8,128)(2,1)} %bitcast.9, s32[6,2,24]{2,1,0:T(2,128)} %bitcast.10, bf16[320,288]{1,0:T(8,128)(2,1)} %constant.6.clone.perm_hbm.perm_ref, ...), custom_call_target="tpu_custom_call" | custom-call | tf_op jit(solution)/shard_map/block/pallas_call | solution.py:568
  55.5 0.0 copy-done
  55.5 2.6 %finish.1 = (bf16[288,512]{1,0:T(8,128)(2,1)}, bf16[288,512]{1,0:T(8,128)(2,1)}, f32[512,1536]{1,0:T(8,128)}, f32[512,512]{1,0:T(8,128)}, f32[1,512]{1,0:T(1,128)}, /*index=5*/f32[1,8]{1,0:T(1,128)}) custom-call(bf16[8,80,512]{2,1,0:T(8,128)(2,1)S(1)} %get-tuple-element.15.ret_ref, bf16[2,4096,128]{2,1,0:T(8,128)(2,1)S(1)} %get-tuple-element.16.sum_ref, ...), custom_call_target="tpu_custom_call" | custom-call | tf_op jit(solution)/shard_map/finish/pallas_call | solution.py:627
Async XLA Ops:
  0.6 54.9 %copy-start = (bf16[320,288]{1,0:T(8,128)(2,1)S(1)}, bf16[320,288]{1,0:T(8,128)(2,1)}, u32[]{:S(2)}) copy-start(bf16[320,288]{1,0:T(8,128)(2,1)} %constant.6.clone.perm_hbm.perm_ref) | copy-start | bytes 552964

commit v6 on v2

--- a/solution.py
+++ b/solution.py
@@ -132,6 +132,8 @@
         ("scale", scale_hbm, scale_ref),
     )):
         loads[name] = pltpu.make_async_copy(src, dst, w_sem.at[i])
+    first_loads = ("x", "perm", "keep", "member", "place", "g")
+    for name in first_loads:
         loads[name].start()
 
     barrier = pltpu.get_barrier_semaphore()
@@ -151,8 +153,10 @@
         started.append(copy)
         return copy
 
-    for name in ("perm", "x", "keep", "member", "place", "g"):
+    for name in first_loads:
         loads[name].wait()
+    for name in ("gain", "qkv", "proj", "scale"):
+        loads[name].start()
     perm = perm_ref[...]
     xs = dot(perm, x_ref[...])
     gs = dot(perm, g_ref[...])
@@ -496,14 +500,19 @@
     advance_wave(1, 0)
     send_back((5, 7, 6, 3))
     for stage in range(1, 7):
+        departed = len(started)
         advance_wave(0, stage)
         advance_wave(1, stage)
         if stage < 4:
             small_copies = small_stage(stage, small_sum(stage - 1, small_copies))
         elif stage == 4:
             small_out_ref[...] = small_sum(3, small_copies)
-    for slot in back:
-        back[slot].wait_recv()
+            for slot in back:
+                back[slot].wait_recv()
+        if stage < 6:
+            for copy in started[:departed]:
+                copy.wait_send()
+            del started[:departed]
     for copy in started:
         copy.wait_send()
 

time: 55.8 us -> 55.6 us (level)
  no operation moved by 1% of the time
where the time goes in v6:
time: 55.6 us; the launch traced here: 55.5 us
  Pallas kernels  54.8 us (99%)
  between operations  0.66 us (1%)
    pallas_call x1, Pallas kernels, per_device(): pl.pallas_call(block_kernel, out_shape=(jax.ShapeDtypeStruct((8, ROWS, 51...  52.2 us
    pallas_call x1, Pallas kernels, per_device(): pl.pallas_call(finish_kernel, out_shape=(jax.ShapeDtypeStruct((288, 512),...  2.62 us

profile of v6, /device:TPU:1, one launch (start us, length us, event | category | flops | bytes accessed | tf_op | source)
XLA Modules:
  0.0 55.5 jit_solution(6304258585495278163)
XLA Ops:
  0.6 0.0 copy-start
  0.6 52.2 %block.1 = (bf16[8,80,512]{2,1,0:T(8,128)(2,1)S(1)}, bf16[2,4096,128]{2,1,0:T(8,128)(2,1)S(1)}, f32[16,128]{1,0:T(8,128)S(1)}) custom-call(bf16[288,512]{1,0:T(8,128)(2,1)} %bitcast.8, bf16[288,512]{1,0:T(8,128)(2,1)} %bitcast.9, s32[6,2,24]{2,1,0:T(2,128)} %bitcast.10, bf16[320,288]{1,0:T(8,128)(2,1)} %constant.6.clone.perm_hbm.perm_ref, ...), custom_call_target="tpu_custom_call" | custom-call | tf_op jit(solution)/shard_map/block/pallas_call | solution.py:563
  52.8 0.0 copy-done
  52.9 2.6 %finish.1 = (bf16[288,512]{1,0:T(8,128)(2,1)}, bf16[288,512]{1,0:T(8,128)(2,1)}, f32[512,1536]{1,0:T(8,128)}, f32[512,512]{1,0:T(8,128)}, f32[1,512]{1,0:T(1,128)}, /*index=5*/f32[1,8]{1,0:T(1,128)}) custom-call(bf16[8,80,512]{2,1,0:T(8,128)(2,1)S(1)} %get-tuple-element.15.ret_ref, bf16[2,4096,128]{2,1,0:T(8,128)(2,1)S(1)} %get-tuple-element.16.sum_ref, ...), custom_call_target="tpu_custom_call" | custom-call | tf_op jit(solution)/shard_map/finish/pallas_call | solution.py:622
Async XLA Ops:
  0.6 52.2 %copy-start = (bf16[320,288]{1,0:T(8,128)(2,1)S(1)}, bf16[320,288]{1,0:T(8,128)(2,1)}, u32[]{:S(2)}) copy-start(bf16[320,288]{1,0:T(8,128)(2,1)} %constant.6.clone.perm_hbm.perm_ref) | copy-start | bytes 552964

commit v7 on v6

--- a/solution.py
+++ b/solution.py
@@ -59,12 +59,12 @@
 KEPT_SLOTS = (0, 1, 4)
 
 GROUPS = (
-    (0, 768, "xzy"),
-    (768, 512, "yxz"),
-    (1280, 768, "zyx"),
-    (2048, 768, "xzy"),
-    (2816, 512, "yxz"),
-    (3328, 768, "zyx"),
+    (0, 704, "xzy"),
+    (704, 640, "yxz"),
+    (1344, 704, "zyx"),
+    (2048, 704, "xzy"),
+    (2752, 640, "yxz"),
+    (3392, 704, "zyx"),
 )
 WAVES = ((0, 1, 2), (3, 4, 5))
 
@@ -107,7 +107,7 @@
     ret_ref, sum_ref, small_out_ref,
     x_ref, g_ref, keep_ref, perm_ref, member_ref, place_ref, wqkv_ref, wproj_ref, gain_ref, scale_ref, in_buf, win_ref, back_ref,
     x_s, xh_s, rstd_s, y_s, g_s, rq_s, rk_s, rq_rows_s, q_s, k_s, qd_s, kd_s, v_s, do_s, dq_s, dk_s, dv_s, att_s, allow_s, gs_s, small_s,
-    grads_ref, r0, a1, r1, a2, r2, a3, sv0, sv1, sv2, sv3,
+    grads_ref, r0, a1, r1, a2, a3, sv0, sv1, sv2, sv3,
     w_sem, in_send, in_recv, out_send, out_recv, sib_send, sib_recv, st_send, st_recv, sv_send, sv_recv,
 ):
     lat, lon = position()
@@ -283,43 +283,28 @@
         for copy in flight[group]:
             copy.wait_recv()
 
-    def size_of(group, level):
-        return GROUPS[group][1] // (4, 16)[level]
-
-    def start_of(group, level):
-        return GROUPS[group][0] // (1, 4)[level]
-
-    def own_rows(group, level, j=0):
-        first, size = start_of(group, level), size_of(group, level)
-        turn = lax.rem(co[GROUPS[group][2][level]] + j, 4)
+    def own_rows(group, j=0):
+        first, rows, axes = GROUPS[group]
+        size = rows // 4
+        turn = lax.rem(co[axes[0]] + j, 4)
         return pl.ds(pl.multiple_of(first + turn * size, 16), size)
 
-    def landing(group, level):
-        return pl.ds(GROUPS[group][0] // (4, 16)[level], size_of(group, level))
-
-    def scatter(group, level, src, dst):
-        def pairs(j):
-            return src.at[own_rows(group, level, j + 1)], dst.at[j, landing(group, level)]
-
-        send_stage(group, level, GROUPS[group][2][level], pairs)
-
-    def gathered(group, level, src, dst):
+    def landing(group):
+        return pl.ds(GROUPS[group][0] // 4, GROUPS[group][1] // 4)
+
+    def exchange(group, stage, buf, total):
+        axis = GROUPS[group][2][stage]
+        me = co[axis]
+        buf[me, landing(group)] = total.astype(BF)
+        here = buf.at[me, landing(group)]
+        send_stage(group, stage, axis, lambda j: (here, here))
+
+    def exchanged(group, buf):
         arrived(group)
-        total = src[own_rows(group, level)].astype(F32)
-        for j in range(3):
-            total = total + dst[j, landing(group, level)].astype(F32)
-        return total.astype(BF)
-
-    def final_rows(group, level):
-        first, rows, axes = GROUPS[group]
-        off = first + co[axes[0]] * (rows // 4)
-        if level == 1:
-            off = off + co[axes[1]] * (rows // 16)
-        return pl.ds(pl.multiple_of(off, 16), size_of(group, level))
-
-    def spread(group, level):
-        where = sum_ref.at[core, final_rows(group, level)]
-        send_stage(group, 4 - level, GROUPS[group][2][level], lambda j: (where, where))
+        total = buf[0, landing(group)].astype(F32)
+        for i in range(1, 4):
+            total = total + buf[i, landing(group)].astype(F32)
+        return total
 
     sib_in = {}
 
@@ -334,26 +319,22 @@
 
     def advance(group, stage):
         if stage == 0:
-            scatter(group, 0, a1, r1)
+            send_stage(
+                group, 0, GROUPS[group][2][0], lambda j: (a1.at[own_rows(group, j + 1)], r1.at[j, landing(group)])
+            )
         elif stage == 1:
-            a2[landing(group, 0)] = gathered(group, 0, a1, r1)
-            scatter(group, 1, a2, r2)
+            arrived(group)
+            total = a1[own_rows(group)].astype(F32)
+            for j in range(3):
+                total = total + r1[j, landing(group)].astype(F32)
+            exchange(group, 1, a2, total)
         elif stage == 2:
-            me = co[GROUPS[group][2][2]]
-            a3[me, landing(group, 1)] = gathered(group, 1, a2, r2)
-            here = a3.at[me, landing(group, 1)]
-            send_stage(group, 2, GROUPS[group][2][2], lambda j: (here, here))
+            exchange(group, 2, a3, exchanged(group, a2))
         elif stage == 3:
-            arrived(group)
-            total = a3[0, landing(group, 1)].astype(F32)
-            for i in range(1, 4):
-                total = total + a3[i, landing(group, 1)].astype(F32)
-            sum_ref[core, final_rows(group, 1)] = total.astype(BF)
-            spread(group, 1)
+            sum_ref[core, own_rows(group)] = exchanged(group, a3).astype(BF)
+            where = sum_ref.at[core, own_rows(group)]
+            send_stage(group, 3, GROUPS[group][2][0], lambda j: (where, where))
         elif stage == 4:
-            arrived(group)
-            spread(group, 0)
-        elif stage == 5:
             arrived(group)
             whole = sum_ref.at[core, pl.ds(GROUPS[group][0], GROUPS[group][1])]
             flight[group] = [send(whole, whole, sib_send.at[4 + group], sib_recv.at[4 + group], sib)]
@@ -499,7 +480,7 @@
     join(3)
     advance_wave(1, 0)
     send_back((5, 7, 6, 3))
-    for stage in range(1, 7):
+    for stage in range(1, 6):
         departed = len(started)
         advance_wave(0, stage)
         advance_wave(1, stage)
@@ -509,7 +490,7 @@
             small_out_ref[...] = small_sum(3, small_copies)
             for slot in back:
                 back[slot].wait_recv()
-        if stage < 6:
+        if stage < 5:
             for copy in started[:departed]:
                 copy.wait_send()
             del started[:departed]
@@ -601,9 +582,8 @@
             pltpu.VMEM((4096, 128), BF),
             pltpu.VMEM((4096, 128), BF),
             pltpu.VMEM((3, 1024, 128), BF),
-            pltpu.VMEM((1024, 128), BF),
-            pltpu.VMEM((3, 256, 128), BF),
-            pltpu.VMEM((4, 256, 128), BF),
+            pltpu.VMEM((4, 1024, 128), BF),
+            pltpu.VMEM((4, 1024, 128), BF),
             pltpu.VMEM((2, 16, 128), F32),
             pltpu.VMEM((4, 16, 128), F32),
             pltpu.VMEM((4, 16, 128), F32),
@@ -612,7 +592,7 @@
             DMA((5,)), DMA((5,)),
             DMA((5,)), DMA((5,)),
             DMA((10,)), DMA((10,)),
-            DMA((6, 5, 3)), DMA((6, 5, 3)),
+            DMA((6, 4, 3)), DMA((6, 4, 3)),
             DMA((10,)), DMA((10,)),
         ],
         compiler_params=pltpu.CompilerParams(collective_id=1, has_side_effects=True, vmem_limit_bytes=40 * MIB),

time: 55.6 us -> 56.5 us (1.016)
  Pallas kernels: 54.8 us -> 55.7 us
    pallas_call x1, Pallas kernels: 52.2 us -> 53.1 us  [per_device(): pl.pallas_call(block_kernel, out_shape=(jax.ShapeDtypeStruct((8, ROWS, 51...]
where the time goes in v7:
time: 56.5 us; the launch traced here: 56.4 us
  Pallas kernels  55.7 us (99%)
  between operations  0.66 us (1%)
    pallas_call x1, Pallas kernels, per_device(): pl.pallas_call(block_kernel, out_shape=(jax.ShapeDtypeStruct((8, ROWS, 51...  53.1 us
    pallas_call x1, Pallas kernels, per_device(): pl.pallas_call(finish_kernel, out_shape=(jax.ShapeDtypeStruct((288, 512),...  2.62 us

profile of v7, /device:TPU:1, one launch (start us, length us, event | category | flops | bytes accessed | tf_op | source)
XLA Modules:
  0.0 56.4 jit_solution(1905762803733646342)
XLA Ops:
  0.6 0.0 copy-start
  0.6 53.1 %block.1 = (bf16[8,80,512]{2,1,0:T(8,128)(2,1)S(1)}, bf16[2,4096,128]{2,1,0:T(8,128)(2,1)S(1)}, f32[16,128]{1,0:T(8,128)S(1)}) custom-call(bf16[288,512]{1,0:T(8,128)(2,1)} %bitcast.8, bf16[288,512]{1,0:T(8,128)(2,1)} %bitcast.9, s32[6,2,24]{2,1,0:T(2,128)} %bitcast.10, bf16[320,288]{1,0:T(8,128)(2,1)} %constant.6.clone.perm_hbm.perm_ref, ...), custom_call_target="tpu_custom_call" | custom-call | tf_op jit(solution)/shard_map/block/pallas_call | solution.py:544
  53.7 0.0 copy-done
  53.8 2.6 %finish.1 = (bf16[288,512]{1,0:T(8,128)(2,1)}, bf16[288,512]{1,0:T(8,128)(2,1)}, f32[512,1536]{1,0:T(8,128)}, f32[512,512]{1,0:T(8,128)}, f32[1,512]{1,0:T(1,128)}, /*index=5*/f32[1,8]{1,0:T(1,128)}) custom-call(bf16[8,80,512]{2,1,0:T(8,128)(2,1)S(1)} %get-tuple-element.15.ret_ref, bf16[2,4096,128]{2,1,0:T(8,128)(2,1)S(1)} %get-tuple-element.16.sum_ref, ...), custom_call_target="tpu_custom_call" | custom-call | tf_op jit(solution)/shard_map/finish/pallas_call | solution.py:602
Async XLA Ops:
  0.6 53.1 %copy-start = (bf16[320,288]{1,0:T(8,128)(2,1)S(1)}, bf16[320,288]{1,0:T(8,128)(2,1)}, u32[]{:S(2)}) copy-start(bf16[320,288]{1,0:T(8,128)(2,1)} %constant.6.clone.perm_hbm.perm_ref) | copy-start | bytes 552964

commit v8 on v6

--- a/solution.py
+++ b/solution.py
@@ -436,6 +436,8 @@
             join(0)
             join(1)
             advance_wave(0, 0)
+        elif pair == 3:
+            join(2)
 
     def out_slot(slot, pieces):
         back_ref[slot] = jnp.concatenate(pieces, axis=0).astype(BF)
@@ -484,6 +486,8 @@
         return total
 
     small_copies = small_stage(0, small_s[...])
+    join(3)
+    advance_wave(1, 0)
     dxh = dn * gain
     rstd = rstd_s[:, 0:1]
     dx = rstd * (dxh - jnp.mean(dxh, axis=-1, keepdims=True) - xhat * jnp.mean(dxh * xhat, axis=-1, keepdims=True))
@@ -495,9 +499,6 @@
         out_slot(slot, [mixed[rows], gtok[rows]])
     for slot in KEPT_SLOTS:
         ret_ref[slot] = back_ref[slot]
-    join(2)
-    join(3)
-    advance_wave(1, 0)
     send_back((5, 7, 6, 3))
     for stage in range(1, 7):
         departed = len(started)

time: 55.6 us -> 55.9 us (level)
  no operation moved by 1% of the time
where the time goes in v8:
time: 55.9 us; the launch traced here: 55.8 us
  Pallas kernels  55.1 us (99%)
  between operations  0.66 us (1%)
    pallas_call x1, Pallas kernels, per_device(): pl.pallas_call(block_kernel, out_shape=(jax.ShapeDtypeStruct((8, ROWS, 51...  52.5 us
    pallas_call x1, Pallas kernels, per_device(): pl.pallas_call(finish_kernel, out_shape=(jax.ShapeDtypeStruct((288, 512),...  2.62 us

profile of v8, /device:TPU:1, one launch (start us, length us, event | category | flops | bytes accessed | tf_op | source)
XLA Modules:
  0.0 55.8 jit_solution(3640902957178968063)
XLA Ops:
  0.6 0.0 copy-start
  0.6 52.5 %block.1 = (bf16[8,80,512]{2,1,0:T(8,128)(2,1)S(1)}, bf16[2,4096,128]{2,1,0:T(8,128)(2,1)S(1)}, f32[16,128]{1,0:T(8,128)S(1)}) custom-call(bf16[288,512]{1,0:T(8,128)(2,1)} %bitcast.8, bf16[288,512]{1,0:T(8,128)(2,1)} %bitcast.9, s32[6,2,24]{2,1,0:T(2,128)} %bitcast.10, bf16[320,288]{1,0:T(8,128)(2,1)} %constant.6.clone.perm_hbm.perm_ref, ...), custom_call_target="tpu_custom_call" | custom-call | tf_op jit(solution)/shard_map/block/pallas_call | solution.py:564
  53.2 0.0 copy-done
  53.2 2.6 %finish.1 = (bf16[288,512]{1,0:T(8,128)(2,1)}, bf16[288,512]{1,0:T(8,128)(2,1)}, f32[512,1536]{1,0:T(8,128)}, f32[512,512]{1,0:T(8,128)}, f32[1,512]{1,0:T(1,128)}, /*index=5*/f32[1,8]{1,0:T(1,128)}) custom-call(bf16[8,80,512]{2,1,0:T(8,128)(2,1)S(1)} %get-tuple-element.15.ret_ref, bf16[2,4096,128]{2,1,0:T(8,128)(2,1)S(1)} %get-tuple-element.16.sum_ref, ...), custom_call_target="tpu_custom_call" | custom-call | tf_op jit(solution)/shard_map/finish/pallas_call | solution.py:623
Async XLA Ops:
  0.6 52.5 %copy-start = (bf16[320,288]{1,0:T(8,128)(2,1)S(1)}, bf16[320,288]{1,0:T(8,128)(2,1)}, u32[]{:S(2)}) copy-start(bf16[320,288]{1,0:T(8,128)(2,1)} %constant.6.clone.perm_hbm.perm_ref) | copy-start | bytes 552964
